TPU v7x, 32 devices: a whole 2x2x4 slice. The times are simulated.
32 devices in a mesh: gx: 4 (over y, x), yz: 8 (over z, core).
Axes of the slice: x: 2, y: 2, z: 4, core: 2. Of those that a mesh axis runs over, the one named last changes fastest.
Arguments:
- tokens: bfloat16 [4, 256, 18432], P('gx', None, 'yz'), may hold values from -6 to 6
- gain: float32 [18432], replicated, may hold values from 0.1 to 1.9
- w_query: bfloat16 [18432, 8192], P('gx', 'yz'), may hold values from -0.046875 to 0.046875
- w_keyval: bfloat16 [18432, 512], P('gx', 'yz'), may hold values from -0.09375 to 0.09375
- w_out: bfloat16 [8192, 18432], P('gx', 'yz'), may hold values from -0.375 to 0.375
- cache: bfloat16 [4, 2048, 512], P('gx', 'yz'), as said below
- lengths: int32 [4], P('gx'), may hold values from 1024 to 2048, as said below
Outputs:
- attended: bfloat16 [4, 256, 18432], P('gx', None, 'yz')
Inputs may be any that keep to these rules, and one draw needn't show every extreme that they name: `lengths`: some sequence has exactly 2048 filled slots and some exactly 1024. `cache`: cached keys are already rotated to their slot positions.
All inputs are finite; a program needn't handle non-finite values.
Results may differ from a plain program's by a relative error of at most 0.012.
The roundings to bfloat16 on the way count: a program that leaves them out, or rounds other values in their place, can miss the bound.
Values may be sent and summed in bfloat16 or wider, within the bound.
No kernel may reach another device: no remote copies, remote signals or barrier semaphores. Data moves between devices by JAX's collectives and lax.ppermute only.
A program may use at most 192 MiB of HBM per device.

v0:
```python
import math

import jax
import jax.numpy as jnp
from jax import lax
from jax.sharding import PartitionSpec as P

HEAD = 256


def layer_norm(tokens, gain):
    values = tokens.astype(jnp.float32)
    mean = jnp.mean(values, axis=-1, keepdims=True)
    centered = values - mean
    spread = jnp.mean(centered * centered, axis=-1, keepdims=True)
    return (centered * lax.rsqrt(spread + 1e-06) * gain).astype(jnp.bfloat16)


def rotate(values, positions):
    width = values.shape[-1]
    half = width // 2
    freq = jnp.exp(jnp.arange(half, dtype=jnp.float32) * (-2.0 * math.log(10000.0) / width))
    angles = positions.astype(jnp.float32)[..., None] * freq
    cosine = jnp.cos(angles)[:, :, None, :]
    sine = jnp.sin(angles)[:, :, None, :]
    first = values[..., :half]
    second = values[..., half:]
    return jnp.concatenate(
        [first * cosine - second * sine, second * cosine + first * sine], axis=-1
    )


def absorb(carry, query, keys, values, mask, scale):
    largest, total, summed = carry
    scores = jnp.einsum("rchd,rpd->rhcp", query, keys, preferred_element_type=jnp.float32) * scale
    wide_mask = mask[:, None, :, :]
    block_top = jnp.max(jnp.where(wide_mask, scores, -1e30), axis=-1)
    new_top = jnp.maximum(largest, block_top)
    probs = jnp.exp(jnp.where(wide_mask, scores - new_top[..., None], -jnp.inf))
    factor = jnp.exp(largest - new_top)
    total = total * factor + jnp.sum(probs, axis=-1)
    summed = summed * factor[..., None] + jnp.einsum(
        "rhcp,rpd->rhcd", probs.astype(jnp.bfloat16), values, preferred_element_type=jnp.float32
    )
    return (new_top, total, summed)


def body(tokens, gain, w_query, w_keyval, w_out, cache, lengths):
    rows, span, _ = tokens.shape
    whole = lax.all_gather(tokens, "yz", axis=2, tiled=True)
    normed = layer_norm(whole, gain)
    flat = normed.reshape(rows * span, whole.shape[2])
    query_cols = w_query.shape[1]
    pair_cols = w_keyval.shape[1]
    left = flat
    query_raw = jnp.dot(
        left, lax.all_gather(w_query, "gx", axis=0, tiled=True), preferred_element_type=jnp.float32
    )
    pair_part = jnp.dot(
        left, lax.all_gather(w_keyval, "gx", axis=0, tiled=True), preferred_element_type=jnp.float32
    )
    heads_here = query_cols // HEAD
    steps = jnp.arange(span, dtype=jnp.int32)
    positions = lengths[:, None] + steps[None, :]
    query = rotate(query_raw.reshape(rows, span, heads_here, HEAD), positions).astype(jnp.bfloat16)
    keyval = lax.all_gather(
        pair_part.astype(jnp.bfloat16).reshape(rows, span, pair_cols), "yz", axis=2, tiled=True
    )
    fresh_keys = rotate(keyval[:, :, None, :HEAD].astype(jnp.float32), positions)[
        :, :, 0, :
    ].astype(jnp.bfloat16)
    fresh_values = keyval[:, :, HEAD:]
    scale = 1.0 / math.sqrt(HEAD)
    initial = (
        jnp.full((rows, heads_here, span), -1e30, jnp.float32),
        jnp.zeros((rows, heads_here, span), jnp.float32),
        jnp.zeros((rows, heads_here, span, HEAD), jnp.float32),
    )
    piece = lax.all_gather(cache, "yz", axis=1, tiled=True)
    count = piece.shape[1]
    slots = jnp.arange(count, dtype=jnp.int32)
    usable = slots[None, :] < lengths[:, None]
    mask = jnp.broadcast_to(usable[:, None, :], (rows, span, count))
    carry = absorb(initial, query, piece[:, :, :HEAD], piece[:, :, HEAD:], mask, scale)
    causal = (steps[:, None] >= steps[None, :])[None]
    largest, total, summed = absorb(carry, query, fresh_keys, fresh_values, causal, scale)
    heads_out = (summed / total[..., None]).astype(jnp.bfloat16)
    heads_out = heads_out.transpose(0, 2, 1, 3).reshape(rows * span, query_cols)
    all_heads = lax.all_gather(heads_out, "yz", axis=1, tiled=True)
    left = all_heads
    result = jnp.dot(
        left, lax.all_gather(w_out, "gx", axis=0, tiled=True), preferred_element_type=jnp.float32
    )
    return result.astype(jnp.bfloat16).reshape(rows, span, w_out.shape[1])


def solution(mesh):
    return jax.shard_map(
        body,
        mesh=mesh,
        in_specs=(
            P("gx", None, "yz"),
            P(),
            P("gx", "yz"),
            P("gx", "yz"),
            P("gx", "yz"),
            P("gx", "yz", None),
            P("gx"),
        ),
        out_specs=P("gx", None, "yz"),
        check_vma=False,
    )
```

profile of v0, /device:TPU:0, one launch (start us, length us, event | category | flops | bytes accessed | tf_op | source)
XLA Modules:
  0.0 914.6 jit_solution(3924648850189754573)
XLA Ops:
  6.5 0.7 all-gather.8.cloned.1.call-update
  7.3 0.7 all-gather.14.cloned.1.call-update
  8.1 0.7 all-gather.10.cloned.1.call-update
  8.8 0.5 all-gather.12.cloned.1.call-update
  9.4 0.5 all-gather.18.cloned.1.call-update
  10.7 0.5 multiply_cosine_fusion.1
  11.2 91.2 %all-gather.8.cloned.1.call-done = bf16[1,256,18432]{2,1,0:T(8,128)(2,1)} async-done(((bf16[1,256,2304]{2,1,0:T(8,128)(2,1)}), bf16[1,256,18432]{2,1,0:T(8,128)(2,1)}) %all-gather.8.cloned.1.call-update) | async-done | bytes 9437200 | tf_op jit(solution)/shard_map/all_gather | solution.py:50
  102.4 5.2 convert_reduce_fusion
  107.6 1.1 copy-done
  108.8 2.7 fusion.2
  111.5 28.6 %all-gather.14.cloned.1.call-done = bf16[18432,64]{0,1:T(8,128)(2,1)} async-done(((bf16[4608,64]{0,1:T(8,128)(2,1)}), bf16[18432,64]{0,1:T(8,128)(2,1)}) %all-gather.14.cloned.1.call-update) | async-done | bytes 2359312 | tf_op jit(solution)/shard_map/all_gather | solution.py:60
  140.2 7.7 fusion.31
  147.9 14.4 %all-gather = bf16[256,512]{0,1:T(8,128)(2,1)S(1)} all-gather(bf16[256,64]{0,1:T(8,128)(2,1)S(1)} %fusion.31), channel_id=2, replica_groups=mesh['gx'=4,'yz'=8] {'yz'}, dimensions={1}, use_global_device_ids=true | all-gather | bytes 294912 | tf_op jit(solution)/shard_map/all_gather | solution.py:66
  162.4 0.6 fusion.49
  163.0 312.1 %all-gather.10.cloned.1.call-done = bf16[18432,1024]{1,0:T(8,128)(2,1)} async-done(((bf16[4608,1024]{1,0:T(8,128)(2,1)}), bf16[18432,1024]{1,0:T(8,128)(2,1)}) %all-gather.10.cloned.1.call-update) | async-done | bytes 37748752 | tf_op jit(solution)/shard_map/all_gather | solution.py:57
  475.1 49.9 %copy.8 = bf16[1024,18432]{1,0:T(8,128)(2,1)} copy(bf16[1024,18432]{0,1:T(8,128)(2,1)} %bitcast.98) | data formatting | bytes 75497472 | tf_op jit(solution)/shard_map/dot_general | solution.py:56
  525.0 25.4 %fusion.21 = f32[1,256,4,256]{1,3,2,0:T(8,128)S(1)} fusion(bf16[4,256,18432]{2,1,0:T(8,128)(2,1)} %bitcast.99, bf16[1,256,18432]{2,1,0:T(8,128)(2,1)} %all-gather.8.cloned.1.call-done, f32[18432]{0:T(1024)S(1)} %copy-done.2, f32[256]{0:T(256)S(1)} %add_rsqrt_fusion, f32[256]{0:T(256)S(1)} %broadcast_multiply_fusion), kind=kOutput, calls=%fused_computation.27 | convolution fusion | flops 9687269376 | bytes 48310272 | tf_op jit(solution)/shard_map/dot_general | solution.py:56
  550.9 2.9 fusion.9
  554.0 2.0 fusion.12
  556.0 2.2 fusion.27
  558.2 1.2 fusion.30
  559.5 280.5 %all-gather.18.cloned.1.call-done = bf16[8192,2304]{1,0:T(8,128)(2,1)} async-done(((bf16[2048,2304]{1,0:T(8,128)(2,1)}), bf16[8192,2304]{1,0:T(8,128)(2,1)}) %all-gather.18.cloned.1.call-update) | async-done | bytes 37748752 | tf_op jit(solution)/shard_map/all_gather | solution.py:92
  839.9 48.6 %all-gather.16.cloned.1.call-done = bf16[256,8192]{0,1:T(8,128)(2,1)} async-done(((bf16[256,1024]{0,1:T(8,128)(2,1)}), bf16[256,8192]{0,1:T(8,128)(2,1)}) %all-gather.16.cloned.1.call-update) | async-done | bytes 4194320 | tf_op jit(solution)/shard_map/all_gather | solution.py:89
  888.6 19.2 %fusion.18 = bf16[1,256,2304]{2,1,0:T(8,128)(2,1)} fusion(bf16[256,8192]{0,1:T(8,128)(2,1)} %all-gather.16.cloned.1.call-done, bf16[8192,2304]{1,0:T(8,128)(2,1)} %all-gather.18.cloned.1.call-done), kind=kOutput, calls=%fused_computation.22 | convolution fusion | flops 9664266240 | bytes 43122688 | tf_op jit(solution)/shard_map/dot_general | solution.py:91
  (25 shorter events, 1.0 us)
Async XLA Ops:
  6.5 95.9 %all-gather.8.cloned.1.call-start = ((), (), s32[]{:S(2)}) async-start(), calls=%async_computation | async-start | bytes 10616832 | tf_op jit(solution)/shard_map/all_gather | solution.py:50
  7.3 132.9 %all-gather.14.cloned.1.call-start = ((), (), s32[]{:S(2)}) async-start(), calls=%async_computation.3 | async-start | bytes 2949120 | tf_op jit(solution)/shard_map/all_gather | solution.py:60
  8.0 467.1 %all-gather.10.cloned.1.call-start = ((), (), s32[]{:S(2)}) async-start(), calls=%async_computation.1 | async-start | bytes 47185920 | tf_op jit(solution)/shard_map/all_gather | solution.py:57
  8.7 542.2 %all-gather.12.cloned.1.call-start = ((), (), s32[]{:S(2)}) async-start(), calls=%async_computation.2 | async-start | bytes 2359296 | tf_op jit(solution)/shard_map/all_gather | solution.py:79
  9.3 830.6 %all-gather.18.cloned.1.call-start = ((), (), s32[]{:S(2)}) async-start(), calls=%async_computation.5 | async-start | bytes 47185920 | tf_op jit(solution)/shard_map/all_gather | solution.py:92
  9.9 878.7 %all-gather.16.cloned.1.call-start = ((), (), s32[]{:S(2)}) async-start(), calls=%async_computation.4 | async-start | bytes 4718592 | tf_op jit(solution)/shard_map/all_gather | solution.py:89
  102.4 6.4 copy-start
  102.4 37.8 %copy-start.2 = (f32[18432]{0:T(1024)S(1)}, f32[18432]{0:T(1024)}, u32[]{:S(2)}) copy-start(f32[18432]{0:T(1024)} %param.8) | copy-start | bytes 221188
  550.9 5.1 copy-start.1
Sparse Core Ops, SparseCore 0:
  9.0 93.4 all-gather.7
  104.3 35.8 all-gather.13
  142.1 332.9 all-gather.9
  476.6 29.0 all-gather.11
  507.4 332.4 all-gather.17
  841.4 47.1 all-gather.15
where the time goes:
time: 916 us; the launch traced here: 915 us
  waiting for transfers between devices  764 us (83%)
  matrix products  58.9 us (6%)
  local copies, waits for them, and re-layouts  51 us (6%)
  blocking collectives  14.4 us (2%)
  between operations  14.2 us (2%)
  other arithmetic  11.5 us (1%)
    all_gather x1, waiting for transfers between devices, body(): lax.all_gather(w_query, 'gx', axis=0, tiled=True)  312 us
    all_gather x1, waiting for transfers between devices, body(): lax.all_gather(w_out, 'gx', axis=0, tiled=True)  280 us
    all_gather x1, waiting for transfers between devices, body(): whole = lax.all_gather(tokens, 'yz', axis=2, tiled=True)  91.2 us
    dot_general x1, local copies, waits for them, and re-layouts, body(): jnp.dot(left, lax.all_gather(w_query, 'gx', axis=0, tiled=True), preferre...  49.9 us
    all_gather x1, waiting for transfers between devices, body(): all_heads = lax.all_gather(heads_out, 'yz', axis=1, tiled=True)  48.6 us
    all_gather x1, waiting for transfers between devices, body(): lax.all_gather(w_keyval, 'gx', axis=0, tiled=True)  28.6 us
    dot_general x1, matrix products, body(): jnp.dot(left, lax.all_gather(w_query, 'gx', axis=0, tiled=True), preferre...  25.4 us
    dot_general x1, matrix products, body(): jnp.dot(left, lax.all_gather(w_out, 'gx', axis=0, tiled=True), preferred_...  19.2 us
  transfers between devices with their start and end apart: 6, of which 5 were waited for; matrix products, arithmetic and copies ran while one was open for 11% of the time, Pallas kernels for 0%

commit v1 on v0

v1 whole, which is shorter than its diff:
```python
import functools
import math

import jax
import jax.numpy as jnp
from jax import lax
from jax.experimental import pallas as pl
from jax.experimental.pallas import tpu as pltpu
from jax.sharding import PartitionSpec as P

HEAD = 256
HALF = HEAD // 2
SHARES = (4, 4)
VMEM = 26 << 20
FREE = pl.CostEstimate(flops=0, bytes_accessed=0, transcendentals=0)


def in_hbm(array):
    return pltpu.with_memory_space_constraint(array, pltpu.HBM)


def pick_kernel(parts, index, *refs):
    held, outs, sems = refs[:parts], refs[parts:-1], refs[-1]
    for k, out in enumerate(outs):
        for m, block in enumerate(held):

            @pl.when(index[k] == m)
            def _():
                pltpu.make_async_copy(block, out, sems.at[k]).start()

    for k, out in enumerate(outs):
        pltpu.make_async_copy(held[0], out, sems.at[k]).wait()


def pick(index, held):
    parts = len(held)
    block = held[0]
    return pl.pallas_call(
        functools.partial(pick_kernel, parts),
        grid_spec=pltpu.PrefetchScalarGridSpec(
            num_scalar_prefetch=1,
            grid=(),
            in_specs=[pl.BlockSpec(memory_space=pl.ANY)] * parts,
            out_specs=[pl.BlockSpec(memory_space=pl.ANY)] * parts,
            scratch_shapes=[pltpu.SemaphoreType.DMA((parts,))],
        ),
        out_shape=[jax.ShapeDtypeStruct(block.shape, block.dtype)] * parts,
        compiler_params=pltpu.CompilerParams(vmem_limit_bytes=VMEM),
        cost_estimate=FREE,
    )(index, *held)


def normalise_kernel(parts, index, mean, factor, gains, *refs):
    outs, held, blocks, sems = refs[-2 - parts : -2], refs[: -2 - parts], refs[-2], refs[-1]
    for k in range(parts):
        for m, block in enumerate(held):

            @pl.when(index[k] == m)
            def _():
                pltpu.make_async_copy(block, blocks.at[k], sems.at[k]).start()

    for k, out in enumerate(outs):
        pltpu.make_async_copy(held[0], blocks.at[k], sems.at[k]).wait()
        gain = gains[k : k + 1, :]

        @pl.loop(0, out.shape[0], step=32)
        def _(start):
            rows = pl.ds(pl.multiple_of(start, 32), 32)
            centred = blocks[k, rows, :].astype(jnp.float32) - mean[rows, :]
            out[rows, :] = (centred * factor[rows, :] * gain).astype(out.dtype)


def normalise(index, mean, factor, gains, held):
    parts = index.shape[0]
    block = held[0]
    inside = pl.BlockSpec(memory_space=pltpu.VMEM)
    return pl.pallas_call(
        functools.partial(normalise_kernel, parts),
        grid_spec=pltpu.PrefetchScalarGridSpec(
            num_scalar_prefetch=1,
            grid=(),
            in_specs=[inside] * 3 + [pl.BlockSpec(memory_space=pl.ANY)] * len(held),
            out_specs=[inside] * parts,
            scratch_shapes=[
                pltpu.VMEM((parts, *block.shape), block.dtype),
                pltpu.SemaphoreType.DMA((parts,)),
            ],
        ),
        out_shape=[jax.ShapeDtypeStruct(block.shape, block.dtype)] * parts,
        compiler_params=pltpu.CompilerParams(vmem_limit_bytes=VMEM),
        cost_estimate=FREE,
    )(index, mean, factor, gains, *held)


def join_kernel(*refs):
    *pieces, out, sems = refs
    size = pieces[0].shape[0]
    copies = [
        pltpu.make_async_copy(piece, out.at[pl.ds(i * size, size)], sems.at[i])
        for i, piece in enumerate(pieces)
    ]
    for copy in copies:
        copy.start()
    for copy in copies:
        copy.wait()


def join(pieces):
    size, columns = pieces[0].shape
    return pl.pallas_call(
        join_kernel,
        in_specs=[pl.BlockSpec(memory_space=pl.ANY)] * len(pieces),
        out_specs=pl.BlockSpec(memory_space=pl.ANY),
        scratch_shapes=[pltpu.SemaphoreType.DMA((len(pieces),))],
        out_shape=jax.ShapeDtypeStruct((len(pieces) * size, columns), pieces[0].dtype),
        compiler_params=pltpu.CompilerParams(vmem_limit_bytes=VMEM),
        cost_estimate=FREE,
    )(*pieces)


def tail_kernel(*refs):
    *parts, out = refs
    total = parts[0][...]
    for part in parts[1:]:
        total += part[...].astype(jnp.float32)
    out[...] = total.astype(out.dtype)


def tail_sum(parts, columns):
    size, total = parts[0].shape
    last = total // columns - 1
    return pl.pallas_call(
        tail_kernel,
        grid=(1,),
        in_specs=[pl.BlockSpec((size, columns), lambda i: (0, last))] * len(parts),
        out_specs=pl.BlockSpec((size, columns), lambda i: (0, 0)),
        out_shape=jax.ShapeDtypeStruct((size, columns), jnp.bfloat16),
        compiler_params=pltpu.CompilerParams(vmem_limit_bytes=VMEM),
        cost_estimate=FREE,
    )(*parts)


def widest(columns):
    for width in (768, 512, 256):
        if columns % width == 0:
            return width
    return columns


def product_kernel(groups, joined, which, *refs):
    near_pieces, far_pieces, refs = refs[:groups], refs[groups : groups + joined], refs[groups + joined :]
    weight, refs = refs[0], refs[1:]
    extra, narrow = None, None
    if len(refs) > groups + 4:
        extra, narrow, refs = refs[:2], refs[-1], refs[2:-1]
    outs, (rows, tiles, sums, sems) = refs[:groups], refs[groups:]
    blocks, _, deep = rows.shape
    size, depth = near_pieces[0].shape
    columns = weight.shape[1]
    shares = blocks // 2
    width = widest(columns)

    waits = []
    for block in range(blocks):
        half, share = block // shares, block % shares
        mine = half == 0
        row = pl.multiple_of((which[0] if mine else 1 - which[0]) * depth + share * deep, deep)
        part = slice(share * deep, (share + 1) * deep)
        pieces = near_pieces if mine else far_pieces
        tall = groups * size // len(pieces)
        moves = [
            (piece.at[:, part], rows.at[block, pl.ds(i * tall, tall)]) for i, piece in enumerate(pieces)
        ]
        moves.append((weight.at[pl.ds(row, deep)], tiles.at[block]))
        if extra is not None:
            for other, source in enumerate(extra):
                high = source.shape[0]
                place = which[0] if other == 0 else 1 - which[0]
                moves.append(
                    (
                        source.at[:, pl.ds(row, deep)],
                        narrow.at[block, pl.ds(pl.multiple_of(place * high, high), high)],
                    )
                )
        waits.append(
            [pltpu.make_async_copy(a, b, sems.at[block, i]) for i, (a, b) in enumerate(moves)]
        )
    for copies in waits:
        for copy in copies:
            copy.start()

    def add(total, place, block):
        if block:
            total += sums[:, place]
        if block < blocks - 1:
            sums[:, place] = total
        else:
            for k, out in enumerate(outs):
                out[:, place] = total[k * size : (k + 1) * size].astype(out.dtype)

    for block, copies in enumerate(waits):
        for copy in copies:
            copy.wait()
        if extra is not None:
            total = lax.dot_general(
                rows[block], narrow[block], (((1,), (1,)), ((), ())), preferred_element_type=jnp.float32
            )
            add(total, slice(columns, None), block)

        @pl.loop(0, columns // width)
        def _(j):
            place = pl.ds(pl.multiple_of(j * width, width), width)
            total = jnp.dot(rows[block], tiles[block, :, place], preferred_element_type=jnp.float32)
            add(total, place, block)


def product(which, own, other, weight, extra=None):
    groups = len(own)
    size, depth = own[0].shape
    columns = weight.shape[1]
    shares = 2 if depth % 256 == 0 and depth > 1024 else 1
    deep = depth // shares
    weights = [weight]
    total = columns
    if extra is not None:
        weights += extra
        total += 2 * extra[0].shape[0]
    scratch = [
        pltpu.VMEM((2 * shares, groups * size, deep), jnp.bfloat16),
        pltpu.VMEM((2 * shares, deep, columns), jnp.bfloat16),
        pltpu.VMEM((groups * size, total), jnp.float32),
        pltpu.SemaphoreType.DMA((2 * shares, groups + 3)),
    ]
    if extra is not None:
        scratch.append(pltpu.VMEM((2 * shares, total - columns, deep), jnp.bfloat16))
    operands = [*own, *other, *map(in_hbm, weights)]
    return pl.pallas_call(
        functools.partial(product_kernel, groups, len(other)),
        grid_spec=pltpu.PrefetchScalarGridSpec(
            num_scalar_prefetch=1,
            grid=(),
            in_specs=[pl.BlockSpec(memory_space=pl.ANY)] * len(operands),
            out_specs=[pl.BlockSpec(memory_space=pltpu.VMEM)] * groups,
            scratch_shapes=scratch,
        ),
        out_shape=[
            jax.ShapeDtypeStruct((size, total), jnp.bfloat16 if k else jnp.float32) for k in range(groups)
        ],
        compiler_params=pltpu.CompilerParams(vmem_limit_bytes=VMEM),
        cost_estimate=FREE,
    )(which, *operands)


def attend_kernel(sizes, heads, parts, info, *refs):
    chunk = len(sizes) - 1
    size = sizes[-1]
    starts = [sum(sizes[:c]) for c in range(len(sizes))]
    count = parts + 3 + parts * (chunk + 1)
    sources, out, held = refs[:count], refs[count], refs[count + 1 : -3]
    keys, values, sems = refs[-3:]
    queries, held = held[:parts], held[parts:]
    cosine, sine, past = held[:3]
    pairs = held[3:]
    length = info[0]
    z = info[1]
    step = pl.program_id(0)

    def turned(first, second, rows):
        cos = cosine[rows, :]
        sin = sine[rows, :]
        return first * cos - second * sin, second * cos + first * sin

    @pl.when(step == 0)
    def _():
        copies = [
            pltpu.make_async_copy(source, target, sems.at[i])
            for i, (source, target) in enumerate(zip(sources, refs[count + 1 : -3]))
        ]
        for copy in copies:
            copy.start()
        for copy in copies:
            copy.wait()
        for c in range(chunk + 1):
            rows = slice(starts[c], starts[c] + sizes[c])
            found = []
            for a in range(parts):
                block = pairs[c * parts][...]
                for k in range(1, parts):
                    block = jnp.where(z == a ^ k, pairs[c * parts + k][...], block)
                found.append(block)
            joined = jnp.concatenate(found, axis=1)
            first, second = turned(
                joined[:, :HALF].astype(jnp.float32), joined[:, HALF:HEAD].astype(jnp.float32), rows
            )
            keys[rows, :HALF] = first.astype(jnp.bfloat16)
            keys[rows, HALF:] = second.astype(jnp.bfloat16)
            values[rows, :] = joined[:, HEAD:]

    here = pl.ds(pl.multiple_of(step * (heads * HEAD), heads * HEAD), heads * HEAD)
    raw = queries[0][:, here]
    for k in range(1, parts):
        raw = raw + queries[k][:, here].astype(jnp.float32)
    asked = []
    for h in range(heads):
        first, second = turned(
            raw[:, h * HEAD : h * HEAD + HALF],
            raw[:, h * HEAD + HALF : (h + 1) * HEAD],
            slice(starts[-1], starts[-1] + size),
        )
        asked.append(jnp.concatenate([first.astype(jnp.bfloat16), second.astype(jnp.bfloat16)], axis=1))
    query = jnp.concatenate(asked, axis=0)
    scale = 1.0 / math.sqrt(HEAD)
    dims = (((1,), (1,)), ((), ()))
    old = lax.dot_general(query, past[:, :HEAD], dims, preferred_element_type=jnp.float32) * scale
    new = lax.dot_general(query, keys[...], dims, preferred_element_type=jnp.float32) * scale
    slot = lax.broadcasted_iota(jnp.int32, (1, old.shape[1]), 1)
    old = jnp.where(slot < length, old, -jnp.inf)
    row = lax.broadcasted_iota(jnp.int32, new.shape, 0) % size + starts[-1]
    column = lax.broadcasted_iota(jnp.int32, new.shape, 1)
    new = jnp.where(column <= row, new, -jnp.inf)
    top = jnp.maximum(jnp.max(old, axis=1, keepdims=True), jnp.max(new, axis=1, keepdims=True))
    old = jnp.exp(old - top)
    new = jnp.exp(new - top)
    total = jnp.sum(old, axis=1, keepdims=True) + jnp.sum(new, axis=1, keepdims=True)
    summed = jnp.dot(old.astype(jnp.bfloat16), past[:, HEAD:], preferred_element_type=jnp.float32)
    summed += jnp.dot(new.astype(jnp.bfloat16), values[...], preferred_element_type=jnp.float32)
    result = (summed / total).astype(jnp.bfloat16)
    for h in range(heads):
        out[:, h * HEAD : (h + 1) * HEAD] = result[h * size : (h + 1) * size]


def attend(info, queries, cosine, sine, past, pairs):
    parts = len(queries)
    size = queries[0].shape[0]
    columns = queries[0].shape[1] - pairs[0][0].shape[1]
    heads = columns // HEAD
    at_once = 2 if heads % 2 == 0 else 1
    operands = [*queries, cosine, sine, past, *[p for group in pairs for p in group]]
    sizes = tuple(group[0].shape[0] for group in pairs)
    fresh = sum(sizes)
    return pl.pallas_call(
        functools.partial(attend_kernel, sizes, at_once, parts),
        grid_spec=pltpu.PrefetchScalarGridSpec(
            num_scalar_prefetch=1,
            grid=(heads // at_once,),
            in_specs=[pl.BlockSpec(memory_space=pl.ANY)] * len(operands),
            out_specs=pl.BlockSpec((size, at_once * HEAD), lambda h, w: (0, h)),
            scratch_shapes=[pltpu.VMEM(a.shape, a.dtype) for a in operands]
            + [
                pltpu.VMEM((fresh, HEAD), jnp.bfloat16),
                pltpu.VMEM((fresh, HEAD), jnp.bfloat16),
                pltpu.SemaphoreType.DMA((len(operands),)),
            ],
        ),
        out_shape=jax.ShapeDtypeStruct((size, columns), jnp.bfloat16),
        compiler_params=pltpu.CompilerParams(vmem_limit_bytes=VMEM),
        cost_estimate=FREE,
    )(info, *queries, *map(in_hbm, operands[parts : parts + 3]), *operands[parts + 3 :])


def solution(mesh):
    n_gx = mesh.shape["gx"]
    n_yz = mesh.shape["yz"]
    inner = n_yz // n_gx
    groups = [[z * inner + r for r in range(inner)] for z in range(n_gx)]
    swap = [(j, j ^ 1) for j in range(n_yz)]

    def tie(value, earlier):
        return lax.optimization_barrier((value, earlier))[0]

    def hop(block, k):
        pairs = [(a * inner + b, (a ^ k) * inner + b) for a in range(n_gx) for b in range(inner)]
        return lax.ppermute(block, "yz", pairs)

    def around(block, end=n_gx):
        return complete([block], end)

    def complete(held, end=n_gx):
        held = list(held)
        for m in range(len(held), end):
            low = m & -m
            block = held[m - low]
            held.append(hop(tie(block, held[1:m]) if m != low else block, low))
        return held

    def turn(picks):
        return [exchange(block, k) for k, block in enumerate(picks)]

    def exchange(block, k):
        if k == 0:
            return block
        return lax.ppermute(block, "gx", [(s, s ^ k) for s in range(n_gx)])

    def times(rows, other, which, weight, extra=None):
        if inner == 2:
            return product(which, rows, other, weight, extra)
        if extra is not None:
            weight = jnp.concatenate([weight, extra], axis=1)
        out = jnp.dot(other, weight, preferred_element_type=jnp.float32)
        out = out.reshape(n_gx, -1, weight.shape[1])
        return [out[0]] + [out[k].astype(jnp.bfloat16) for k in range(1, n_gx)]

    def partner(rows, joined):
        if inner == 2:
            if joined == 1:
                rows = [tie(rows[0], rows[1]), *rows[1:]]
            else:
                rows = [join(rows[i : i + joined]) for i in range(0, n_gx, joined)]
            return [lax.ppermute(block, "yz", swap) for block in rows]
        rows = jnp.concatenate(rows, axis=0)
        return lax.all_gather(rows, "yz", axis=1, tiled=True, axis_index_groups=groups)

    def give(partial):
        return [exchange(p, k) for k, p in enumerate(partial)]

    def collect(partial):
        total = partial[0]
        for p in partial[1:]:
            total = total + p.astype(jnp.float32)
        return total.astype(jnp.bfloat16)

    def pair_columns(part, r):
        if inner == 2:
            other = lax.ppermute(part, "yz", swap)
            return jnp.concatenate(
                [jnp.where(r == 0, part, other), jnp.where(r == 0, other, part)], axis=1
            )
        return lax.all_gather(part, "yz", axis=1, tiled=True, axis_index_groups=groups)

    def across(part):
        return [part] + [hop(part, k) for k in range(1, n_gx)]

    def body(tokens, gain, w_query, w_keyval, w_out, cache, lengths):
        gx = lax.axis_index("gx")
        yz = lax.axis_index("yz")
        z = yz // inner
        r = yz % inner
        _, span, width = tokens.shape
        features = width * n_yz
        n_yz_columns = w_keyval.shape[1]
        ends = [span * sum(SHARES[: t + 1]) // sum(SHARES) for t in range(len(SHARES))]
        parts = [slice(start, end) for start, end in zip([0] + ends, ends)]
        length = lengths[0]

        first = around(tokens[0, parts[0]])

        values = tokens[0].astype(jnp.float32)
        mine = jnp.mean(values, axis=-1)
        moment = jnp.sum(jnp.square(values - mine[:, None]), axis=-1)
        stats = pair_columns(jnp.stack([mine, moment])[:, None], r)
        stats = jnp.concatenate(across(stats), axis=1)
        mean = jnp.mean(stats[0], axis=0)
        moments = jnp.sum(stats[1], axis=0) + width * jnp.sum(
            jnp.square(stats[0] - mean), axis=0
        )
        factor = lax.rsqrt(moments / features + 1e-06)
        gains = gain.reshape(n_gx, inner, width)[gx ^ jnp.arange(n_gx), r]
        if inner == 2:
            w_keyval = w_keyval.T
            w_keyval = [w_keyval, lax.ppermute(tie(w_keyval, first[3]), "yz", swap)]
        else:
            w_keyval = pair_columns(w_keyval, r)

        which = r[None]
        info = jnp.stack([length, z])
        freq = jnp.exp(jnp.arange(HALF, dtype=jnp.float32) * (-2.0 * math.log(10000.0) / HEAD))
        positions = length + jnp.arange(span, dtype=jnp.int32)
        angles = positions.astype(jnp.float32)[:, None] * freq
        cosine = jnp.cos(angles)
        sine = jnp.sin(angles)

        index = z ^ gx ^ jnp.arange(n_gx, dtype=jnp.int32)
        order = [range(1, n_gx - 1), [n_gx - 1, 0]]
        shares = [
            (jnp.stack([z ^ gx ^ k for k in ks]), jnp.stack([gains[k] for k in ks])) for ks in order
        ]
        mean, factor, shares = tie(
            (mean[:, None], factor[:, None], shares), (cosine, sine, info, which, index)
        )

        def normalised(t, held, earlier=()):
            picks = {}
            for ks, (some, scale) in zip(order, shares):
                blocks = normalise(some, mean[parts[t]], factor[parts[t]], scale, held)
                picks.update(zip(ks, blocks))
                held = tie(held, (blocks, earlier))
            return [picks[k] for k in range(n_gx)]

        pairs = []

        def fresh(queries):
            columns = inner * n_yz_columns
            return across(tail_sum(queries, columns))

        second = around(tie(tokens[0, parts[1]], first[3]))
        rows = turn(normalised(0, first))
        past = lax.all_gather(tie(cache, (second[1:3], rows[1:])), "yz", axis=1, tiled=True)[0]
        rows[-1] = tie(rows[-1], second[1:3])
        partial = times(rows, partner(rows, 1), which, w_query, w_keyval)
        queries = give(partial)
        pairs.append(fresh(queries))

        picks = normalised(1, tie(second, partial[0]), queries)
        rows = turn(picks)
        heads = attend(info, tie(queries, picks[0]), cosine, sine, past, pairs)
        first = around(heads)

        rows = tie(rows, first[1:3])
        other = partner(rows, 2)
        picks = pick(index, first)
        first_rows = turn(picks)
        rows, other = tie((rows, other), picks)
        partial = times(rows, other, which, w_query, w_keyval)
        queries = give(partial)

        rows = tie(first_rows, partial[0])
        partial = times(rows, partner(rows, 4), which, w_out)
        outs = [give(partial)]

        queries = tie(queries, partial[0])
        pairs.append(fresh(queries))
        heads = attend(info, queries, cosine, sine, past, pairs)
        rows = turn(pick(index, tie(around(heads), outs[0][1:])))
        outs.append(give(times(rows, partner(rows, 4), which, w_out)))
        outs = [collect(o) for o in outs]
        return jnp.concatenate(outs, axis=0)[None]

    return jax.shard_map(
        body,
        mesh=mesh,
        in_specs=(
            P("gx", None, "yz"),
            P(),
            P("gx", "yz"),
            P("gx", "yz"),
            P("gx", "yz"),
            P("gx", "yz", None),
            P("gx"),
        ),
        out_specs=P("gx", None, "yz"),
        check_vma=False,
    )
```

time: 916 us -> 301 us (0.33)
  waiting for transfers between devices: 764 us -> 146 us
  Pallas kernels: 0 us -> 62.5 us
  matrix products: 58.9 us -> 0 us
  starting transfers between devices: 0.19 us -> 57.9 us
  local copies, waits for them, and re-layouts: 51 us -> 15 us
  blocking collectives: 14.4 us -> 0 us
    all_gather x6 -> x1, waiting for transfers between devices: 761 us -> 0.01 us  [body(): lax.all_gather(tie(cache, (second[1:3], rows[1:])), 'yz', axis=1, tiled=T...]
    ppermute x0 -> x55, waiting for transfers between devices: none -> 146 us  [the longest x21 85.2 us: hop(): return lax.ppermute(block, 'yz', pairs)]
    pallas_call x0 -> x18, Pallas kernels: none -> 62.5 us  [the longest x4 38.5 us: product(): pl.pallas_call(functools.partial(product_kernel, groups, len(other)), gri...]
    dot_general x7 -> x0, matrix products: 58.9 us -> none  [the longest x1 25.4 us: body(): jnp.dot(left, lax.all_gather(w_query, 'gx', axis=0, tiled=True), preferre...]
    ppermute x0 -> x55, starting transfers between devices: none -> 57.9 us  [the longest x24 28.4 us: exchange(): return lax.ppermute(block, 'gx', [(s, s ^ k) for s in range(n_gx)])]
    dot_general x1 -> x0, local copies, waits for them, and re-layouts: 49.9 us -> none  [body(): jnp.dot(left, lax.all_gather(w_query, 'gx', axis=0, tiled=True), preferre...]
    all_gather x1 -> x0, blocking collectives: 14.4 us -> none  [body(): lax.all_gather(pair_part.astype(jnp.bfloat16).reshape(rows, span, pair_co...]
    reduce_sum x4, other arithmetic: 10.1 us -> 0.73 us  [the longest x1 0.46 us: body(): moment = jnp.sum(jnp.square(values - mine[:, None]), axis=-1)]
  transfers between devices with their start and end apart: 6 -> 56, of which waited for: 5 -> 29; matrix products, arithmetic and copies ran while one was open for 11% -> 2% of each run, Pallas kernels for 0% -> 17%
where the time goes in v1:
time: 301 us
  waiting for transfers between devices  146 us (49%)
  Pallas kernels  62.5 us (21%)
  starting transfers between devices  57.9 us (19%)
  local copies, waits for them, and re-layouts  15 us (5%)
  between operations  14.6 us (5%)
  other arithmetic  4.43 us (1%)
    ppermute x21, waiting for transfers between devices, hop(): return lax.ppermute(block, 'yz', pairs)  85.2 us
    ppermute x24, waiting for transfers between devices, exchange(): return lax.ppermute(block, 'gx', [(s, s ^ k) for s in range(n_gx)])  55.1 us
    pallas_call x4, Pallas kernels, product(): pl.pallas_call(functools.partial(product_kernel, groups, len(other)), gri...  38.5 us
    ppermute x24, starting transfers between devices, exchange(): return lax.ppermute(block, 'gx', [(s, s ^ k) for s in range(n_gx)])  28.4 us
    ppermute x21, starting transfers between devices, hop(): return lax.ppermute(block, 'yz', pairs)  27.4 us
    pallas_call x2, Pallas kernels, attend(): pl.pallas_call(functools.partial(attend_kernel, sizes, at_once, parts), g...  12.9 us
    unnamed x52, local copies, waits for them, and re-layouts  10.4 us
    pallas_call x4, Pallas kernels, normalise(): pl.pallas_call(functools.partial(normalise_kernel, parts), grid_spec=pltp...  8.65 us
  transfers between devices with their start and end apart: 56, of which 29 were waited for; matrix products, arithmetic and copies ran while one was open for 2% of the time, Pallas kernels for 17%

profile of v1, /device:TPU:0, one launch (start us, length us, event | category | flops | bytes accessed | tf_op | source)
XLA Modules:
  0.0 300.6 jit_solution(16276325939773534458)
XLA Ops:
  8.0 3.1 %collective-permute-start.4 = (bf16[128,2304]{1,0:T(8,128)(2,1)S(1)}, bf16[128,2304]{1,0:T(8,128)(2,1)S(1)}, u32[]{:S(2)}, u32[]{:S(2)}) collective-permute-start(bf16[128,2304]{1,0:T(8,128)(2,1)S(1)} %get-tuple-element.99.refs_0_), channel_id=1, source_target_pairs={{0,2},{1,3},{2,0},{3,1},{4,6},{5,7},{6,4},{7,5},{8,10},{9,11},{10,... | collective-permute-start | bytes 1769480 | tf_op jit(solution)/shard_map/ppermute | solution.py:373
  19.3 3.9 %collective-permute-start.3 = (f32[2,2,256]{2,1,0:T(2,128)S(1)}, f32[2,2,256]{2,1,0:T(2,128)S(1)}, u32[]{:S(2)}, u32[]{:S(2)}) collective-permute-start(f32[2,2,256]{2,1,0:T(2,128)S(1)} %pad_maximum_fusion.1), channel_id=1, source_target_pairs={{0,6},{1,7},{2,4},{3,5},{4,2},{5,3},{6,0},{7,1},{8,14},{9,15},{10,... | collective-permute-start | bytes 12296 | tf_op jit(solution)/shard_map/ppermute | solution.py:373
  23.3 13.7 %collective-permute-done.1 = f32[2,2,256]{2,1,0:T(2,128)S(1)} collective-permute-done((f32[2,2,256]{2,1,0:T(2,128)S(1)}, f32[2,2,256]{2,1,0:T(2,128)S(1)}, u32[]{:S(2)}, u32[]{:S(2)}) %collective-permute-start.1) | collective-permute-done | bytes 4128 | tf_op jit(solution)/shard_map/ppermute | solution.py:373
  42.1 11.5 %collective-permute-done.6.refs_3_ = bf16[128,2304]{1,0:T(8,128)(2,1)S(1)} collective-permute-done((bf16[128,2304]{1,0:T(8,128)(2,1)S(1)}, bf16[128,2304]{1,0:T(8,128)(2,1)S(1)}, u32[]{:S(2)}, u32[]{:S(2)}) %collective-permute-start.6) | collective-permute-done | bytes 589856 | tf_op jit(solution)/shard_map/ppermute | solution.py:373
  63.4 8.3 %collective-permute-done.7.refs_1_ = bf16[128,2304]{1,0:T(8,128)(2,1)S(1)} collective-permute-done((bf16[128,2304]{1,0:T(8,128)(2,1)S(1)}, bf16[128,2304]{1,0:T(8,128)(2,1)S(1)}, u32[]{:S(2)}, u32[]{:S(2)}) %collective-permute-start.7) | collective-permute-done | bytes 589856 | tf_op jit(solution)/shard_map/ppermute | solution.py:392
  71.7 10.2 %collective-permute-done.9.refs_3_ = bf16[128,2304]{1,0:T(8,128)(2,1)S(1)} collective-permute-done((bf16[128,2304]{1,0:T(8,128)(2,1)S(1)}, bf16[128,2304]{1,0:T(8,128)(2,1)S(1)}, u32[]{:S(2)}, u32[]{:S(2)}) %collective-permute-start.9) | collective-permute-done | bytes 589856 | tf_op jit(solution)/shard_map/ppermute | solution.py:392
  83.5 3.9 %collective-permute-done.11.refs_2_ = bf16[128,2304]{1,0:T(8,128)(2,1)S(1)} collective-permute-done((bf16[128,2304]{1,0:T(8,128)(2,1)S(1)}, bf16[128,2304]{1,0:T(8,128)(2,1)S(1)}, u32[]{:S(2)}, u32[]{:S(2)}) %collective-permute-start.11) | collective-permute-done | bytes 589856 | tf_op jit(solution)/shard_map/ppermute | solution.py:373
  96.3 10.7 %shard_map.75 = (f32[128,1152]{1,0:T(8,128)S(1)}, bf16[128,1152]{1,0:T(8,128)(2,1)S(1)}, bf16[128,1152]{1,0:T(8,128)(2,1)S(1)}, bf16[128,1152]{1,0:T(8,128)(2,1)S(1)}) custom-call(s32[1]{0:T(128)} %bitcast.which, bf16[128,2304]{1,0:T(8,128)(2,1)S(1)} %copy-done.11, bf16[128,2304]{1,0:T(8,128)(2,1)S(1)} %copy-done.9, ...), custom_call_target="tpu_custom_call" | custom-call | tf_op jit(solution)/shard_map/pallas_call | solution.py:237
  110.6 11.4 %collective-permute-done.20.refs_3_ = bf16[128,2304]{1,0:T(8,128)(2,1)S(1)} collective-permute-done((bf16[128,2304]{1,0:T(8,128)(2,1)S(1)}, bf16[128,2304]{1,0:T(8,128)(2,1)S(1)}, u32[]{:S(2)}, u32[]{:S(2)}) %collective-permute-start.20) | collective-permute-done | bytes 589856 | tf_op jit(solution)/shard_map/ppermute | solution.py:373
  138.4 3.5 %collective-permute-done.23.refs_10_ = bf16[128,128]{1,0:T(8,128)(2,1)S(1)} collective-permute-done((bf16[128,128]{1,0:T(8,128)(2,1)S(1)}, bf16[128,128]{1,0:T(8,128)(2,1)S(1)}, u32[]{:S(2)}, u32[]{:S(2)}) %collective-permute-start.23) | collective-permute-done | bytes 32800 | tf_op jit(solution)/shard_map/ppermute | solution.py:373
  144.7 6.3 %shard_map.79.refs_0_ = bf16[128,1024]{1,0:T(8,128)(2,1)S(1)} custom-call(s32[2]{0:T(128)S(1)} %get-tuple-element.189.info, f32[128,1152]{1,0:T(8,128)S(1)} %get-tuple-element.125.refs_0_, bf16[128,1152]{1,0:T(8,128)(2,1)S(1)} %copy-done.3, bf16[128,1152]{1,0:T(8,128)(2,1)S(1)} %copy-done.5, bf16[128,1152]{1,0:T(8,128)(2,1)S(1)} %copy-done.7, ...), custom_call_target="tpu_custom_call" | custom-call | tf_op jit(solution)/shard_map/pallas_call | solution.py:341
  155.1 6.1 %collective-permute-done.24.refs_1_ = bf16[128,1024]{1,0:T(8,128)(2,1)S(1)} collective-permute-done((bf16[128,1024]{1,0:T(8,128)(2,1)S(1)}, bf16[128,1024]{1,0:T(8,128)(2,1)S(1)}, u32[]{:S(2)}, u32[]{:S(2)}) %collective-permute-start.24) | collective-permute-done | bytes 262176 | tf_op jit(solution)/shard_map/ppermute | solution.py:373
  163.5 8.3 %collective-permute-done.26.refs_3_ = bf16[128,1024]{1,0:T(8,128)(2,1)S(1)} collective-permute-done((bf16[128,1024]{1,0:T(8,128)(2,1)S(1)}, bf16[128,1024]{1,0:T(8,128)(2,1)S(1)}, u32[]{:S(2)}, u32[]{:S(2)}) %collective-permute-start.26) | collective-permute-done | bytes 262176 | tf_op jit(solution)/shard_map/ppermute | solution.py:373
  176.3 10.7 %shard_map.83 = (f32[128,1152]{1,0:T(8,128)S(1)}, bf16[128,1152]{1,0:T(8,128)(2,1)S(1)}, bf16[128,1152]{1,0:T(8,128)(2,1)S(1)}, bf16[128,1152]{1,0:T(8,128)(2,1)S(1)}) custom-call(s32[1]{0:T(128)} %bitcast.which, bf16[128,2304]{1,0:T(8,128)(2,1)S(1)} %get-tuple-element.140.refs_0_, bf16[128,2304]{1,0:T(8,128)(2,1)S(1)} %collective-permute-done.30.refs_1_, ...), custom_call_target="tpu_custom_call" | custom-call | tf_op jit(solution)/shard_map/pallas_call | solution.py:237
  190.9 8.5 %shard_map.85 = (f32[128,2304]{1,0:T(8,128)S(1)}, bf16[128,2304]{1,0:T(8,128)(2,1)S(1)}, bf16[128,2304]{1,0:T(8,128)(2,1)S(1)}, bf16[128,2304]{1,0:T(8,128)(2,1)S(1)}) custom-call(s32[1]{0:T(128)} %bitcast.which, bf16[128,1024]{1,0:T(8,128)(2,1)S(1)} %get-tuple-element.147.refs_0_, bf16[128,1024]{1,0:T(8,128)(2,1)S(1)} %collective-permute-done.27.refs_1_, ...), custom_call_target="tpu_custom_call" | custom-call | tf_op jit(solution)/shard_map/pallas_call | solution.py:237
  199.4 4.8 %collective-permute-done.40.refs_2_ = bf16[128,1152]{1,0:T(8,128)(2,1)S(1)} collective-permute-done((bf16[128,1152]{1,0:T(8,128)(2,1)S(1)}, bf16[128,1152]{1,0:T(8,128)(2,1)S(1)}, u32[]{:S(2)}, u32[]{:S(2)}) %collective-permute-start.40) | collective-permute-done | bytes 294944 | tf_op jit(solution)/shard_map/ppermute | solution.py:392
  212.9 3.4 %collective-permute-done.44.refs_14_ = bf16[128,128]{1,0:T(8,128)(2,1)S(1)} collective-permute-done((bf16[128,128]{1,0:T(8,128)(2,1)S(1)}, bf16[128,128]{1,0:T(8,128)(2,1)S(1)}, u32[]{:S(2)}, u32[]{:S(2)}) %collective-permute-start.44) | collective-permute-done | bytes 32800 | tf_op jit(solution)/shard_map/ppermute | solution.py:373
  216.4 6.5 %shard_map.87.refs_0_ = bf16[128,1024]{1,0:T(8,128)(2,1)S(1)} custom-call(s32[2]{0:T(128)S(1)} %get-tuple-element.189.info, f32[128,1152]{1,0:T(8,128)S(1)} %get-tuple-element.158.refs_0_, bf16[128,1152]{1,0:T(8,128)(2,1)S(1)} %collective-permute-done.39.refs_1_, bf16[128,1152]{1,0:T(8,128)(2,1)S(1)} %collective-permute-done.40.refs_2_, ...), custom_call_target="tpu_custom_call" | custom-call | tf_op jit(solution)/shard_map/pallas_call | solution.py:341
  225.1 7.9 %collective-permute-done.45.refs_1_ = bf16[128,1024]{1,0:T(8,128)(2,1)S(1)} collective-permute-done((bf16[128,1024]{1,0:T(8,128)(2,1)S(1)}, bf16[128,1024]{1,0:T(8,128)(2,1)S(1)}, u32[]{:S(2)}, u32[]{:S(2)}) %collective-permute-start.45) | collective-permute-done | bytes 262176 | tf_op jit(solution)/shard_map/ppermute | solution.py:373
  234.8 6.4 %collective-permute-done.47.refs_3_ = bf16[128,1024]{1,0:T(8,128)(2,1)S(1)} collective-permute-done((bf16[128,1024]{1,0:T(8,128)(2,1)S(1)}, bf16[128,1024]{1,0:T(8,128)(2,1)S(1)}, u32[]{:S(2)}, u32[]{:S(2)}) %collective-permute-start.47) | collective-permute-done | bytes 262176 | tf_op jit(solution)/shard_map/ppermute | solution.py:373
  248.4 3.2 %collective-permute-done.49.refs_2_ = bf16[128,1024]{1,0:T(8,128)(2,1)S(1)} collective-permute-done((bf16[128,1024]{1,0:T(8,128)(2,1)S(1)}, bf16[128,1024]{1,0:T(8,128)(2,1)S(1)}, u32[]{:S(2)}, u32[]{:S(2)}) %collective-permute-start.49) | collective-permute-done | bytes 262176 | tf_op jit(solution)/shard_map/ppermute | solution.py:392
  254.4 8.5 %shard_map.90 = (f32[128,2304]{1,0:T(8,128)S(1)}, bf16[128,2304]{1,0:T(8,128)(2,1)S(1)}, bf16[128,2304]{1,0:T(8,128)(2,1)S(1)}, bf16[128,2304]{1,0:T(8,128)(2,1)S(1)}) custom-call(s32[1]{0:T(128)} %bitcast.which, bf16[128,1024]{1,0:T(8,128)(2,1)S(1)} %get-tuple-element.167.refs_0_, bf16[128,1024]{1,0:T(8,128)(2,1)S(1)} %collective-permute-done.48.refs_1_, ...), custom_call_target="tpu_custom_call" | custom-call | tf_op jit(solution)/shard_map/pallas_call | solution.py:237
  266.7 12.4 %collective-permute-done.52 = bf16[128,2304]{1,0:T(8,128)(2,1)S(1)} collective-permute-done((bf16[128,2304]{1,0:T(8,128)(2,1)S(1)}, bf16[128,2304]{1,0:T(8,128)(2,1)S(1)}, u32[]{:S(2)}, u32[]{:S(2)}) %collective-permute-start.52) | collective-permute-done | bytes 589856 | tf_op jit(solution)/shard_map/ppermute | solution.py:392
  279.2 13.2 %collective-permute-done.53 = bf16[128,2304]{1,0:T(8,128)(2,1)S(1)} collective-permute-done((bf16[128,2304]{1,0:T(8,128)(2,1)S(1)}, bf16[128,2304]{1,0:T(8,128)(2,1)S(1)}, u32[]{:S(2)}, u32[]{:S(2)}) %collective-permute-start.53) | collective-permute-done | bytes 589856 | tf_op jit(solution)/shard_map/ppermute | solution.py:392
  (191 shorter events, 99.6 us)
Async XLA Ops:
  6.5 135.3 %all-gather.2.cloned.1.call-start = ((), (), s32[]{:S(2)}) async-start(), calls=%async_computation | async-start | bytes 2359296 | tf_op jit(solution)/shard_map/all_gather | solution.py:497
  8.0 31.9 %collective-permute-start.4 = (bf16[128,2304]{1,0:T(8,128)(2,1)S(1)}, bf16[128,2304]{1,0:T(8,128)(2,1)S(1)}, u32[]{:S(2)}, u32[]{:S(2)}) collective-permute-start(bf16[128,2304]{1,0:T(8,128)(2,1)S(1)} %get-tuple-element.99.refs_0_), channel_id=1, source_target_pairs={{0,2},{1,3},{2,0},{3,1},{4,6},{5,7},{6,4},{7,5},{8,10},{9,11},{10,... | collective-permute-start | bytes 1769480 | tf_op jit(solution)/shard_map/ppermute | solution.py:373
  11.0 28.8 %collective-permute-start.5 = (bf16[128,2304]{1,0:T(8,128)(2,1)S(1)}, bf16[128,2304]{1,0:T(8,128)(2,1)S(1)}, u32[]{:S(2)}, u32[]{:S(2)}) collective-permute-start(bf16[128,2304]{1,0:T(8,128)(2,1)S(1)} %get-tuple-element.99.refs_0_), channel_id=1, source_target_pairs={{0,4},{1,5},{2,6},{3,7},{4,0},{5,1},{6,2},{7,3},{8,12},{9,13},{10,... | collective-permute-start | bytes 1769480 | tf_op jit(solution)/shard_map/ppermute | solution.py:373
  18.7 18.2 %collective-permute-start.1 = (f32[2,2,256]{2,1,0:T(2,128)S(1)}, f32[2,2,256]{2,1,0:T(2,128)S(1)}, u32[]{:S(2)}, u32[]{:S(2)}) collective-permute-start(f32[2,2,256]{2,1,0:T(2,128)S(1)} %pad_maximum_fusion.1), channel_id=1, source_target_pairs={{0,2},{1,3},{2,0},{3,1},{4,6},{5,7},{6,4},{7,5},{8,10},{9,11},{10,... | collective-permute-start | bytes 12296 | tf_op jit(solution)/shard_map/ppermute | solution.py:373
  19.2 20.5 %collective-permute-start.2 = (f32[2,2,256]{2,1,0:T(2,128)S(1)}, f32[2,2,256]{2,1,0:T(2,128)S(1)}, u32[]{:S(2)}, u32[]{:S(2)}) collective-permute-start(f32[2,2,256]{2,1,0:T(2,128)S(1)} %pad_maximum_fusion.1), channel_id=1, source_target_pairs={{0,4},{1,5},{2,6},{3,7},{4,0},{5,1},{6,2},{7,3},{8,12},{9,13},{10,... | collective-permute-start | bytes 12296 | tf_op jit(solution)/shard_map/ppermute | solution.py:373
  19.3 20.5 %collective-permute-start.3 = (f32[2,2,256]{2,1,0:T(2,128)S(1)}, f32[2,2,256]{2,1,0:T(2,128)S(1)}, u32[]{:S(2)}, u32[]{:S(2)}) collective-permute-start(f32[2,2,256]{2,1,0:T(2,128)S(1)} %pad_maximum_fusion.1), channel_id=1, source_target_pairs={{0,6},{1,7},{2,4},{3,5},{4,2},{5,3},{6,0},{7,1},{8,14},{9,15},{10,... | collective-permute-start | bytes 12296 | tf_op jit(solution)/shard_map/ppermute | solution.py:373
  55.4 16.3 %collective-permute-start.7 = (bf16[128,2304]{1,0:T(8,128)(2,1)S(1)}, bf16[128,2304]{1,0:T(8,128)(2,1)S(1)}, u32[]{:S(2)}, u32[]{:S(2)}) collective-permute-start(bf16[128,2304]{1,0:T(8,128)(2,1)S(1)} %get-tuple-element.97), channel_id=1, source_target_pairs={{0,8},{8,0},{16,24},{24,16},{1,9},{9,1},{17,25},{25,17},{2,10},{10... | collective-permute-start | bytes 1769480 | tf_op jit(solution)/shard_map/ppermute | solution.py:392
  59.5 22.4 %collective-permute-start.9 = (bf16[128,2304]{1,0:T(8,128)(2,1)S(1)}, bf16[128,2304]{1,0:T(8,128)(2,1)S(1)}, u32[]{:S(2)}, u32[]{:S(2)}) collective-permute-start(bf16[128,2304]{1,0:T(8,128)(2,1)S(1)} %get-tuple-element.104), channel_id=1, source_target_pairs={{0,24},{8,16},{16,8},{24,0},{1,25},{9,17},{17,9},{25,1},{2,26},{10... | collective-permute-start | bytes 1769480 | tf_op jit(solution)/shard_map/ppermute | solution.py:392
  61.0 22.5 %collective-permute-start.10 = (bf16[128,2304]{1,0:T(8,128)(2,1)S(1)}, bf16[128,2304]{1,0:T(8,128)(2,1)S(1)}, u32[]{:S(2)}, u32[]{:S(2)}) collective-permute-start(bf16[128,2304]{1,0:T(8,128)(2,1)S(1)} %get-tuple-element.120.refs_0_), channel_id=1, source_target_pairs={{0,2},{1,3},{2,0},{3,1},{4,6},{5,7},{6,4},{7,5},{8,10},{9,11},{10,... | collective-permute-start | bytes 1769480 | tf_op jit(solution)/shard_map/ppermute | solution.py:373
  61.8 25.7 %collective-permute-start.11 = (bf16[128,2304]{1,0:T(8,128)(2,1)S(1)}, bf16[128,2304]{1,0:T(8,128)(2,1)S(1)}, u32[]{:S(2)}, u32[]{:S(2)}) collective-permute-start(bf16[128,2304]{1,0:T(8,128)(2,1)S(1)} %get-tuple-element.120.refs_0_), channel_id=1, source_target_pairs={{0,4},{1,5},{2,6},{3,7},{4,0},{5,1},{6,2},{7,3},{8,12},{9,13},{10,... | collective-permute-start | bytes 1769480 | tf_op jit(solution)/shard_map/ppermute | solution.py:373
  62.9 24.5 %collective-permute-start.8 = (bf16[128,2304]{1,0:T(8,128)(2,1)S(1)}, bf16[128,2304]{1,0:T(8,128)(2,1)S(1)}, u32[]{:S(2)}, u32[]{:S(2)}) collective-permute-start(bf16[128,2304]{1,0:T(8,128)(2,1)S(1)} %get-tuple-element.98), channel_id=1, source_target_pairs={{0,16},{8,24},{16,0},{24,8},{1,17},{9,25},{17,1},{25,9},{2,18},{10... | collective-permute-start | bytes 1769480 | tf_op jit(solution)/shard_map/ppermute | solution.py:392
  89.7 32.2 %collective-permute-start.20 = (bf16[128,2304]{1,0:T(8,128)(2,1)S(1)}, bf16[128,2304]{1,0:T(8,128)(2,1)S(1)}, u32[]{:S(2)}, u32[]{:S(2)}) collective-permute-start(bf16[128,2304]{1,0:T(8,128)(2,1)S(1)} %collective-permute-done.11.refs_2_), channel_id=1, source_target_pairs={{0,2},{1,3},{2,0},{3,1},{4,6},{5,7},{6,4},{7,5},{8,10},{9,11},{10,... | collective-permute-start | bytes 1769480 | tf_op jit(solution)/shard_map/ppermute | solution.py:373
  107.0 19.4 %collective-permute-start.17 = (bf16[128,1152]{1,0:T(8,128)(2,1)S(1)}, bf16[128,1152]{1,0:T(8,128)(2,1)S(1)}, u32[]{:S(2)}, u32[]{:S(2)}) collective-permute-start(bf16[128,1152]{1,0:T(8,128)(2,1)S(1)} %get-tuple-element.110), channel_id=1, source_target_pairs={{0,8},{8,0},{16,24},{24,16},{1,9},{9,1},{17,25},{25,17},{2,10},{10... | collective-permute-start | bytes 884744 | tf_op jit(solution)/shard_map/ppermute | solution.py:392
  108.4 18.0 %collective-permute-start.18 = (bf16[128,1152]{1,0:T(8,128)(2,1)S(1)}, bf16[128,1152]{1,0:T(8,128)(2,1)S(1)}, u32[]{:S(2)}, u32[]{:S(2)}) collective-permute-start(bf16[128,1152]{1,0:T(8,128)(2,1)S(1)} %get-tuple-element.111), channel_id=1, source_target_pairs={{0,16},{8,24},{16,0},{24,8},{1,17},{9,25},{17,1},{25,9},{2,18},{10... | collective-permute-start | bytes 884744 | tf_op jit(solution)/shard_map/ppermute | solution.py:392
  108.9 17.5 %collective-permute-start.19 = (bf16[128,1152]{1,0:T(8,128)(2,1)S(1)}, bf16[128,1152]{1,0:T(8,128)(2,1)S(1)}, u32[]{:S(2)}, u32[]{:S(2)}) collective-permute-start(bf16[128,1152]{1,0:T(8,128)(2,1)S(1)} %get-tuple-element.112), channel_id=1, source_target_pairs={{0,24},{8,16},{16,8},{24,0},{1,25},{9,17},{17,9},{25,1},{2,26},{10... | collective-permute-start | bytes 884744 | tf_op jit(solution)/shard_map/ppermute | solution.py:392
  124.7 30.3 %collective-permute-start.30 = (bf16[128,2304]{1,0:T(8,128)(2,1)}, bf16[128,2304]{1,0:T(8,128)(2,1)S(1)}, u32[]{:S(2)}, u32[]{:S(2)}) collective-permute-start(bf16[128,2304]{1,0:T(8,128)(2,1)} %get-tuple-element.118), channel_id=1, source_target_pairs={{0,8},{8,0},{16,24},{24,16},{1,9},{9,1},{17,25},{25,17},{2,10},{10... | collective-permute-start | bytes 1769480 | tf_op jit(solution)/shard_map/ppermute | solution.py:392
  126.3 28.8 %collective-permute-start.31 = (bf16[128,2304]{1,0:T(8,128)(2,1)}, bf16[128,2304]{1,0:T(8,128)(2,1)S(1)}, u32[]{:S(2)}, u32[]{:S(2)}) collective-permute-start(bf16[128,2304]{1,0:T(8,128)(2,1)} %get-tuple-element.119), channel_id=1, source_target_pairs={{0,16},{8,24},{16,0},{24,8},{1,17},{9,25},{17,1},{25,9},{2,18},{10... | collective-permute-start | bytes 1769480 | tf_op jit(solution)/shard_map/ppermute | solution.py:392
  130.2 24.8 %collective-permute-start.32 = (bf16[128,2304]{1,0:T(8,128)(2,1)}, bf16[128,2304]{1,0:T(8,128)(2,1)S(1)}, u32[]{:S(2)}, u32[]{:S(2)}) collective-permute-start(bf16[128,2304]{1,0:T(8,128)(2,1)} %get-tuple-element.135), channel_id=1, source_target_pairs={{0,24},{8,16},{16,8},{24,0},{1,25},{9,17},{17,9},{25,1},{2,26},{10... | collective-permute-start | bytes 1769480 | tf_op jit(solution)/shard_map/ppermute | solution.py:392
  204.6 36.5 %collective-permute-start.36 = (bf16[128,2304]{1,0:T(8,128)(2,1)S(1)}, bf16[128,2304]{1,0:T(8,128)(2,1)S(1)}, u32[]{:S(2)}, u32[]{:S(2)}) collective-permute-start(bf16[128,2304]{1,0:T(8,128)(2,1)S(1)} %get-tuple-element.152), channel_id=1, source_target_pairs={{0,8},{8,0},{16,24},{24,16},{1,9},{9,1},{17,25},{25,17},{2,10},{10... | collective-permute-start | bytes 1769480 | tf_op jit(solution)/shard_map/ppermute | solution.py:392
  205.5 35.7 %collective-permute-start.37 = (bf16[128,2304]{1,0:T(8,128)(2,1)S(1)}, bf16[128,2304]{1,0:T(8,128)(2,1)S(1)}, u32[]{:S(2)}, u32[]{:S(2)}) collective-permute-start(bf16[128,2304]{1,0:T(8,128)(2,1)S(1)} %get-tuple-element.153), channel_id=1, source_target_pairs={{0,16},{8,24},{16,0},{24,8},{1,17},{9,25},{17,1},{25,9},{2,18},{10... | collective-permute-start | bytes 1769480 | tf_op jit(solution)/shard_map/ppermute | solution.py:392
  206.4 34.8 %collective-permute-start.38 = (bf16[128,2304]{1,0:T(8,128)(2,1)S(1)}, bf16[128,2304]{1,0:T(8,128)(2,1)S(1)}, u32[]{:S(2)}, u32[]{:S(2)}) collective-permute-start(bf16[128,2304]{1,0:T(8,128)(2,1)S(1)} %get-tuple-element.154), channel_id=1, source_target_pairs={{0,24},{8,16},{16,8},{24,0},{1,25},{9,17},{17,9},{25,1},{2,26},{10... | collective-permute-start | bytes 1769480 | tf_op jit(solution)/shard_map/ppermute | solution.py:392
  262.9 16.2 %collective-permute-start.52 = (bf16[128,2304]{1,0:T(8,128)(2,1)S(1)}, bf16[128,2304]{1,0:T(8,128)(2,1)S(1)}, u32[]{:S(2)}, u32[]{:S(2)}) collective-permute-start(bf16[128,2304]{1,0:T(8,128)(2,1)S(1)} %get-tuple-element.172), channel_id=1, source_target_pairs={{0,8},{8,0},{16,24},{24,16},{1,9},{9,1},{17,25},{25,17},{2,10},{10... | collective-permute-start | bytes 1769480 | tf_op jit(solution)/shard_map/ppermute | solution.py:392
  264.7 27.7 %collective-permute-start.53 = (bf16[128,2304]{1,0:T(8,128)(2,1)S(1)}, bf16[128,2304]{1,0:T(8,128)(2,1)S(1)}, u32[]{:S(2)}, u32[]{:S(2)}) collective-permute-start(bf16[128,2304]{1,0:T(8,128)(2,1)S(1)} %get-tuple-element.173), channel_id=1, source_target_pairs={{0,16},{8,24},{16,0},{24,8},{1,17},{9,25},{17,1},{25,9},{2,18},{10... | collective-permute-start | bytes 1769480 | tf_op jit(solution)/shard_map/ppermute | solution.py:392
  265.2 27.2 %collective-permute-start.54 = (bf16[128,2304]{1,0:T(8,128)(2,1)S(1)}, bf16[128,2304]{1,0:T(8,128)(2,1)S(1)}, u32[]{:S(2)}, u32[]{:S(2)}) collective-permute-start(bf16[128,2304]{1,0:T(8,128)(2,1)S(1)} %get-tuple-element.174), channel_id=1, source_target_pairs={{0,24},{8,16},{16,8},{24,0},{1,25},{9,17},{17,9},{25,1},{2,26},{10... | collective-permute-start | bytes 1769480 | tf_op jit(solution)/shard_map/ppermute | solution.py:392
  (58 other events, 503.7 us)
Sparse Core Ops, SparseCore 0:
  87.6 35.7 all-gather.1

commit v2 on v1

--- a/solution.py
+++ b/solution.py
@@ -12,6 +12,7 @@
 HALF = HEAD // 2
 SHARES = (4, 4)
 VMEM = 26 << 20
+STRIPS = 4
 FREE = pl.CostEstimate(flops=0, bytes_accessed=0, transcendentals=0)
 
 
@@ -171,7 +172,14 @@
         moves = [
             (piece.at[:, part], rows.at[block, pl.ds(i * tall, tall)]) for i, piece in enumerate(pieces)
         ]
-        moves.append((weight.at[pl.ds(row, deep)], tiles.at[block]))
+        strip = deep // STRIPS
+        for i in range(STRIPS):
+            moves.append(
+                (
+                    weight.at[pl.ds(pl.multiple_of(row + i * strip, strip), strip)],
+                    tiles.at[block, pl.ds(i * strip, strip)],
+                )
+            )
         if extra is not None:
             for other, source in enumerate(extra):
                 high = source.shape[0]
@@ -185,9 +193,8 @@
         waits.append(
             [pltpu.make_async_copy(a, b, sems.at[block, i]) for i, (a, b) in enumerate(moves)]
         )
-    for copies in waits:
-        for copy in copies:
-            copy.start()
+    for copy in waits[0] + waits[1]:
+        copy.start()
 
     def add(total, place, block):
         if block:
@@ -201,6 +208,9 @@
     for block, copies in enumerate(waits):
         for copy in copies:
             copy.wait()
+        if block + 2 < blocks:
+            for copy in waits[block + 2]:
+                copy.start()
         if extra is not None:
             total = lax.dot_general(
                 rows[block], narrow[block], (((1,), (1,)), ((), ())), preferred_element_type=jnp.float32
@@ -214,7 +224,7 @@
             add(total, place, block)
 
 
-def product(which, own, other, weight, extra=None):
+def product(which, own, other, weight, extra=None, far=False):
     groups = len(own)
     size, depth = own[0].shape
     columns = weight.shape[1]
@@ -229,10 +239,12 @@
         pltpu.VMEM((2 * shares, groups * size, deep), jnp.bfloat16),
         pltpu.VMEM((2 * shares, deep, columns), jnp.bfloat16),
         pltpu.VMEM((groups * size, total), jnp.float32),
-        pltpu.SemaphoreType.DMA((2 * shares, groups + 3)),
+        pltpu.SemaphoreType.DMA((2 * shares, groups + STRIPS + 2)),
     ]
     if extra is not None:
         scratch.append(pltpu.VMEM((2 * shares, total - columns, deep), jnp.bfloat16))
+    if far:
+        own = map(in_hbm, own)
     operands = [*own, *other, *map(in_hbm, weights)]
     return pl.pallas_call(
         functools.partial(product_kernel, groups, len(other)),
@@ -329,7 +341,7 @@
         out[:, h * HEAD : (h + 1) * HEAD] = result[h * size : (h + 1) * size]
 
 
-def attend(info, queries, cosine, sine, past, pairs):
+def attend(info, queries, cosine, sine, past, pairs, far=False):
     parts = len(queries)
     size = queries[0].shape[0]
     columns = queries[0].shape[1] - pairs[0][0].shape[1]
@@ -355,7 +367,7 @@
         out_shape=jax.ShapeDtypeStruct((size, columns), jnp.bfloat16),
         compiler_params=pltpu.CompilerParams(vmem_limit_bytes=VMEM),
         cost_estimate=FREE,
-    )(info, *queries, *map(in_hbm, operands[parts : parts + 3]), *operands[parts + 3 :])
+    )(info, *(map(in_hbm, queries) if far else queries), *map(in_hbm, operands[parts : parts + 3]), *operands[parts + 3 :])
 
 
 def solution(mesh):
@@ -391,9 +403,9 @@
             return block
         return lax.ppermute(block, "gx", [(s, s ^ k) for s in range(n_gx)])
 
-    def times(rows, other, which, weight, extra=None):
+    def times(rows, other, which, weight, extra=None, far=False):
         if inner == 2:
-            return product(which, rows, other, weight, extra)
+            return product(which, rows, other, weight, extra, far)
         if extra is not None:
             weight = jnp.concatenate([weight, extra], axis=1)
         out = jnp.dot(other, weight, preferred_element_type=jnp.float32)
@@ -437,7 +449,7 @@
         r = yz % inner
         _, span, width = tokens.shape
         features = width * n_yz
-        n_yz_columns = w_keyval.shape[1]
+        pair_columns_here = inner * w_keyval.shape[1]
         ends = [span * sum(SHARES[: t + 1]) // sum(SHARES) for t in range(len(SHARES))]
         parts = [slice(start, end) for start, end in zip([0] + ends, ends)]
         length = lengths[0]
@@ -448,6 +460,12 @@
         mine = jnp.mean(values, axis=-1)
         moment = jnp.sum(jnp.square(values - mine[:, None]), axis=-1)
         stats = pair_columns(jnp.stack([mine, moment])[:, None], r)
+        if inner == 2:
+            w_keyval = w_keyval.T
+            w_keyval = [w_keyval, lax.ppermute(w_keyval, "yz", swap)]
+            stats = tie(stats, w_keyval)
+        else:
+            w_keyval = pair_columns(w_keyval, r)
         stats = jnp.concatenate(across(stats), axis=1)
         mean = jnp.mean(stats[0], axis=0)
         moments = jnp.sum(stats[1], axis=0) + width * jnp.sum(
@@ -455,12 +473,6 @@
         )
         factor = lax.rsqrt(moments / features + 1e-06)
         gains = gain.reshape(n_gx, inner, width)[gx ^ jnp.arange(n_gx), r]
-        if inner == 2:
-            w_keyval = w_keyval.T
-            w_keyval = [w_keyval, lax.ppermute(tie(w_keyval, first[3]), "yz", swap)]
-        else:
-            w_keyval = pair_columns(w_keyval, r)
-
         which = r[None]
         info = jnp.stack([length, z])
         freq = jnp.exp(jnp.arange(HALF, dtype=jnp.float32) * (-2.0 * math.log(10000.0) / HEAD))
@@ -489,20 +501,20 @@
         pairs = []
 
         def fresh(queries):
-            columns = inner * n_yz_columns
-            return across(tail_sum(queries, columns))
+            return across(tail_sum(queries, pair_columns_here))
 
         second = around(tie(tokens[0, parts[1]], first[3]))
         rows = turn(normalised(0, first))
-        past = lax.all_gather(tie(cache, (second[1:3], rows[1:])), "yz", axis=1, tiled=True)[0]
         rows[-1] = tie(rows[-1], second[1:3])
-        partial = times(rows, partner(rows, 1), which, w_query, w_keyval)
+        other = partner(rows, 1)
+        partial = times(rows, other, which, w_query, w_keyval, True)
         queries = give(partial)
         pairs.append(fresh(queries))
 
         picks = normalised(1, tie(second, partial[0]), queries)
+        past = lax.all_gather(tie(cache, picks[1]), "yz", axis=1, tiled=True)[0]
         rows = turn(picks)
-        heads = attend(info, tie(queries, picks[0]), cosine, sine, past, pairs)
+        heads = attend(info, tie(queries, picks[0]), cosine, sine, past, pairs, True)
         first = around(heads)
 
         rows = tie(rows, first[1:3])
@@ -520,7 +532,7 @@
         queries = tie(queries, partial[0])
         pairs.append(fresh(queries))
         heads = attend(info, queries, cosine, sine, past, pairs)
-        rows = turn(pick(index, tie(around(heads), outs[0][1:])))
+        rows = turn(pick(index, tie(around(heads), outs[0][1:3])))
         outs.append(give(times(rows, partner(rows, 4), which, w_out)))
         outs = [collect(o) for o in outs]
         return jnp.concatenate(outs, axis=0)[None]

time: 301 us -> 297 us (0.987)
  local copies, waits for them, and re-layouts: 15 us -> 8.02 us
  waiting for transfers between devices: 146 us -> 151 us
    ppermute x24, waiting for transfers between devices: 55.1 us -> 66.7 us  [exchange(): return lax.ppermute(block, 'gx', [(s, s ^ k) for s in range(n_gx)])]
    unnamed x52 -> x46, local copies, waits for them, and re-layouts: 10.4 us -> 4.71 us
    ppermute x21, waiting for transfers between devices: 85.2 us -> 79.7 us  [hop(): return lax.ppermute(block, 'yz', pairs)]
  transfers between devices with their start and end apart: 56 -> 56, of which waited for: 29 -> 32; matrix products, arithmetic and copies ran while one was open for 2% -> 1% of each run, Pallas kernels for 17% -> 20%
where the time goes in v2:
time: 297 us; the launch traced here: 296 us
  waiting for transfers between devices  151 us (51%)
  Pallas kernels  63.6 us (21%)
  starting transfers between devices  55.6 us (19%)
  between operations  14.6 us (5%)
  local copies, waits for them, and re-layouts  8.02 us (3%)
  other arithmetic  3.88 us (1%)
    ppermute x21, waiting for transfers between devices, hop(): return lax.ppermute(block, 'yz', pairs)  79.7 us
    ppermute x24, waiting for transfers between devices, exchange(): return lax.ppermute(block, 'gx', [(s, s ^ k) for s in range(n_gx)])  66.7 us
    pallas_call x4, Pallas kernels, product(): pl.pallas_call(functools.partial(product_kernel, groups, len(other)), gri...  39.5 us
    ppermute x24, starting transfers between devices, exchange(): return lax.ppermute(block, 'gx', [(s, s ^ k) for s in range(n_gx)])  28.9 us
    ppermute x21, starting transfers between devices, hop(): return lax.ppermute(block, 'yz', pairs)  24.7 us
    pallas_call x2, Pallas kernels, attend(): pl.pallas_call(functools.partial(attend_kernel, sizes, at_once, parts), g...  12.9 us
    pallas_call x4, Pallas kernels, normalise(): pl.pallas_call(functools.partial(normalise_kernel, parts), grid_spec=pltp...  8.64 us
  transfers between devices with their start and end apart: 56, of which 32 were waited for; matrix products, arithmetic and copies ran while one was open for 1% of the time, Pallas kernels for 20%

profile of v2, /device:TPU:0, one launch (start us, length us, event | category | flops | bytes accessed | tf_op | source)
XLA Modules:
  0.0 296.5 jit_solution(10288774019605571475)
XLA Ops:
  8.0 3.1 %collective-permute-start.5 = (bf16[128,2304]{1,0:T(8,128)(2,1)S(1)}, bf16[128,2304]{1,0:T(8,128)(2,1)S(1)}, u32[]{:S(2)}, u32[]{:S(2)}) collective-permute-start(bf16[128,2304]{1,0:T(8,128)(2,1)S(1)} %get-tuple-element.100.refs_0_), channel_id=1, source_target_pairs={{0,2},{1,3},{2,0},{3,1},{4,6},{5,7},{6,4},{7,5},{8,10},{9,11},{10,... | collective-permute-start | bytes 1769480 | tf_op jit(solution)/shard_map/ppermute | solution.py:385
  19.2 3.9 %collective-permute-start.4 = (f32[2,2,256]{2,1,0:T(2,128)S(1)}, f32[2,2,256]{2,1,0:T(2,128)S(1)}, u32[]{:S(2)}, u32[]{:S(2)}) collective-permute-start(f32[2,2,256]{2,1,0:T(2,128)S(1)} %pad_maximum_fusion.2), channel_id=1, source_target_pairs={{0,6},{1,7},{2,4},{3,5},{4,2},{5,3},{6,0},{7,1},{8,14},{9,15},{10,... | collective-permute-start | bytes 12296 | tf_op jit(solution)/shard_map/ppermute | solution.py:385
  23.2 13.7 %collective-permute-done.5.refs_1_ = bf16[128,2304]{1,0:T(8,128)(2,1)S(1)} collective-permute-done((bf16[128,2304]{1,0:T(8,128)(2,1)S(1)}, bf16[128,2304]{1,0:T(8,128)(2,1)S(1)}, u32[]{:S(2)}, u32[]{:S(2)}) %collective-permute-start.5) | collective-permute-done | bytes 589856 | tf_op jit(solution)/shard_map/ppermute | solution.py:385
  40.4 12.0 %collective-permute-done.7.refs_3_ = bf16[128,2304]{1,0:T(8,128)(2,1)S(1)} collective-permute-done((bf16[128,2304]{1,0:T(8,128)(2,1)S(1)}, bf16[128,2304]{1,0:T(8,128)(2,1)S(1)}, u32[]{:S(2)}, u32[]{:S(2)}) %collective-permute-start.7) | collective-permute-done | bytes 589856 | tf_op jit(solution)/shard_map/ppermute | solution.py:385
  62.6 7.9 %collective-permute-done.8.refs_1_ = bf16[128,2304]{1,0:T(8,128)(2,1)S(1)} collective-permute-done((bf16[128,2304]{1,0:T(8,128)(2,1)S(1)}, bf16[128,2304]{1,0:T(8,128)(2,1)S(1)}, u32[]{:S(2)}, u32[]{:S(2)}) %collective-permute-start.8) | collective-permute-done | bytes 589856 | tf_op jit(solution)/shard_map/ppermute | solution.py:404
  70.5 9.7 %collective-permute-done.10.refs_3_ = bf16[128,2304]{1,0:T(8,128)(2,1)S(1)} collective-permute-done((bf16[128,2304]{1,0:T(8,128)(2,1)S(1)}, bf16[128,2304]{1,0:T(8,128)(2,1)S(1)}, u32[]{:S(2)}, u32[]{:S(2)}) %collective-permute-start.10) | collective-permute-done | bytes 589856 | tf_op jit(solution)/shard_map/ppermute | solution.py:404
  81.9 4.6 %collective-permute-done.12.refs_2_ = bf16[128,2304]{1,0:T(8,128)(2,1)S(1)} collective-permute-done((bf16[128,2304]{1,0:T(8,128)(2,1)S(1)}, bf16[128,2304]{1,0:T(8,128)(2,1)S(1)}, u32[]{:S(2)}, u32[]{:S(2)}) %collective-permute-start.12) | collective-permute-done | bytes 589856 | tf_op jit(solution)/shard_map/ppermute | solution.py:385
  90.3 11.3 %shard_map.75 = (f32[128,1152]{1,0:T(8,128)S(1)}, bf16[128,1152]{1,0:T(8,128)(2,1)S(1)}, bf16[128,1152]{1,0:T(8,128)(2,1)S(1)}, bf16[128,1152]{1,0:T(8,128)(2,1)S(1)}) custom-call(s32[1]{0:T(128)} %bitcast.which, bf16[128,2304]{1,0:T(8,128)(2,1)} %copy-done.8, bf16[128,2304]{1,0:T(8,128)(2,1)} %copy-done.20, bf16[128,2304]{1,0:T(8,128)(2,1)} %copy-done.22, ...), custom_call_target="tpu_custom_call" | custom-call | tf_op jit(solution)/shard_map/pallas_call | solution.py:249
  111.1 4.6 %collective-permute-done.17.refs_1_ = bf16[128,1152]{1,0:T(8,128)(2,1)S(1)} collective-permute-done((bf16[128,1152]{1,0:T(8,128)(2,1)}, bf16[128,1152]{1,0:T(8,128)(2,1)S(1)}, u32[]{:S(2)}, u32[]{:S(2)}) %collective-permute-start.17) | collective-permute-done | bytes 294944 | tf_op jit(solution)/shard_map/ppermute | solution.py:404
  115.8 7.6 %collective-permute-done.18.refs_2_ = bf16[128,1152]{1,0:T(8,128)(2,1)S(1)} collective-permute-done((bf16[128,1152]{1,0:T(8,128)(2,1)S(1)}, bf16[128,1152]{1,0:T(8,128)(2,1)S(1)}, u32[]{:S(2)}, u32[]{:S(2)}) %collective-permute-start.18) | collective-permute-done | bytes 294944 | tf_op jit(solution)/shard_map/ppermute | solution.py:404
  137.1 4.3 %collective-permute-done.23.refs_10_ = bf16[128,128]{1,0:T(8,128)(2,1)S(1)} collective-permute-done((bf16[128,128]{1,0:T(8,128)(2,1)S(1)}, bf16[128,128]{1,0:T(8,128)(2,1)S(1)}, u32[]{:S(2)}, u32[]{:S(2)}) %collective-permute-start.23) | collective-permute-done | bytes 32800 | tf_op jit(solution)/shard_map/ppermute | solution.py:385
  141.3 6.4 %shard_map.79.refs_0_ = bf16[128,1024]{1,0:T(8,128)(2,1)S(1)} custom-call(s32[2]{0:T(128)S(1)} %get-tuple-element.189.info, f32[128,1152]{1,0:T(8,128)} %copy-done, bf16[128,1152]{1,0:T(8,128)(2,1)} %copy-done.5, bf16[128,1152]{1,0:T(8,128)(2,1)} %copy-done.6, bf16[128,1152]{1,0:T(8,128)(2,1)} %copy-done.7, f32[256,128]{1,0:T(8,128)} %get-tuple-element.188.refs_4_, ...), custom_call_target="tpu_custom_call" | custom-call | tf_op jit(solution)/shard_map/pallas_call | solution.py:353
  149.3 7.2 %collective-permute-done.24.refs_1_ = bf16[128,1024]{1,0:T(8,128)(2,1)S(1)} collective-permute-done((bf16[128,1024]{1,0:T(8,128)(2,1)S(1)}, bf16[128,1024]{1,0:T(8,128)(2,1)S(1)}, u32[]{:S(2)}, u32[]{:S(2)}) %collective-permute-start.24) | collective-permute-done | bytes 262176 | tf_op jit(solution)/shard_map/ppermute | solution.py:385
  159.1 8.3 %collective-permute-done.26.refs_3_ = bf16[128,1024]{1,0:T(8,128)(2,1)S(1)} collective-permute-done((bf16[128,1024]{1,0:T(8,128)(2,1)S(1)}, bf16[128,1024]{1,0:T(8,128)(2,1)S(1)}, u32[]{:S(2)}, u32[]{:S(2)}) %collective-permute-start.26) | collective-permute-done | bytes 262176 | tf_op jit(solution)/shard_map/ppermute | solution.py:385
  171.9 11.0 %shard_map.83 = (f32[128,1152]{1,0:T(8,128)S(1)}, bf16[128,1152]{1,0:T(8,128)(2,1)S(1)}, bf16[128,1152]{1,0:T(8,128)(2,1)S(1)}, bf16[128,1152]{1,0:T(8,128)(2,1)S(1)}) custom-call(s32[1]{0:T(128)} %bitcast.which, bf16[128,2304]{1,0:T(8,128)(2,1)S(1)} %get-tuple-element.140.refs_0_, bf16[128,2304]{1,0:T(8,128)(2,1)S(1)} %collective-permute-done.30.refs_1_, ...), custom_call_target="tpu_custom_call" | custom-call | tf_op jit(solution)/shard_map/pallas_call | solution.py:249
  186.8 8.6 %shard_map.85 = (f32[128,2304]{1,0:T(8,128)S(1)}, bf16[128,2304]{1,0:T(8,128)(2,1)S(1)}, bf16[128,2304]{1,0:T(8,128)(2,1)S(1)}, bf16[128,2304]{1,0:T(8,128)(2,1)S(1)}) custom-call(s32[1]{0:T(128)} %bitcast.which, bf16[128,1024]{1,0:T(8,128)(2,1)S(1)} %get-tuple-element.147.refs_0_, bf16[128,1024]{1,0:T(8,128)(2,1)S(1)} %collective-permute-done.27.refs_1_, ...), custom_call_target="tpu_custom_call" | custom-call | tf_op jit(solution)/shard_map/pallas_call | solution.py:249
  208.5 6.5 %shard_map.87.refs_0_ = bf16[128,1024]{1,0:T(8,128)(2,1)S(1)} custom-call(s32[2]{0:T(128)S(1)} %get-tuple-element.189.info, f32[128,1152]{1,0:T(8,128)S(1)} %get-tuple-element.158.refs_0_, bf16[128,1152]{1,0:T(8,128)(2,1)S(1)} %collective-permute-done.39.refs_1_, bf16[128,1152]{1,0:T(8,128)(2,1)S(1)} %collective-permute-done.40.refs_2_, ...), custom_call_target="tpu_custom_call" | custom-call | tf_op jit(solution)/shard_map/pallas_call | solution.py:353
  217.8 8.2 %collective-permute-done.45.refs_1_ = bf16[128,1024]{1,0:T(8,128)(2,1)S(1)} collective-permute-done((bf16[128,1024]{1,0:T(8,128)(2,1)S(1)}, bf16[128,1024]{1,0:T(8,128)(2,1)S(1)}, u32[]{:S(2)}, u32[]{:S(2)}) %collective-permute-start.45) | collective-permute-done | bytes 262176 | tf_op jit(solution)/shard_map/ppermute | solution.py:385
  227.6 6.2 %collective-permute-done.47.refs_3_ = bf16[128,1024]{1,0:T(8,128)(2,1)S(1)} collective-permute-done((bf16[128,1024]{1,0:T(8,128)(2,1)S(1)}, bf16[128,1024]{1,0:T(8,128)(2,1)S(1)}, u32[]{:S(2)}, u32[]{:S(2)}) %collective-permute-start.47) | collective-permute-done | bytes 262176 | tf_op jit(solution)/shard_map/ppermute | solution.py:385
  238.2 3.9 %collective-permute-done.48.refs_1_ = bf16[128,1024]{1,0:T(8,128)(2,1)S(1)} collective-permute-done((bf16[128,1024]{1,0:T(8,128)(2,1)S(1)}, bf16[128,1024]{1,0:T(8,128)(2,1)S(1)}, u32[]{:S(2)}, u32[]{:S(2)}) %collective-permute-start.48) | collective-permute-done | bytes 262176 | tf_op jit(solution)/shard_map/ppermute | solution.py:404
  242.1 4.0 %collective-permute-done.49.refs_2_ = bf16[128,1024]{1,0:T(8,128)(2,1)S(1)} collective-permute-done((bf16[128,1024]{1,0:T(8,128)(2,1)S(1)}, bf16[128,1024]{1,0:T(8,128)(2,1)S(1)}, u32[]{:S(2)}, u32[]{:S(2)}) %collective-permute-start.49) | collective-permute-done | bytes 262176 | tf_op jit(solution)/shard_map/ppermute | solution.py:404
  248.9 8.6 %shard_map.90 = (f32[128,2304]{1,0:T(8,128)S(1)}, bf16[128,2304]{1,0:T(8,128)(2,1)S(1)}, bf16[128,2304]{1,0:T(8,128)(2,1)S(1)}, bf16[128,2304]{1,0:T(8,128)(2,1)S(1)}) custom-call(s32[1]{0:T(128)} %bitcast.which, bf16[128,1024]{1,0:T(8,128)(2,1)S(1)} %get-tuple-element.167.refs_0_, bf16[128,1024]{1,0:T(8,128)(2,1)S(1)} %collective-permute-done.48.refs_1_, ...), custom_call_target="tpu_custom_call" | custom-call | tf_op jit(solution)/shard_map/pallas_call | solution.py:249
  263.7 11.4 %collective-permute-done.52 = bf16[128,2304]{1,0:T(8,128)(2,1)S(1)} collective-permute-done((bf16[128,2304]{1,0:T(8,128)(2,1)S(1)}, bf16[128,2304]{1,0:T(8,128)(2,1)S(1)}, u32[]{:S(2)}, u32[]{:S(2)}) %collective-permute-start.52) | collective-permute-done | bytes 589856 | tf_op jit(solution)/shard_map/ppermute | solution.py:404
  276.0 12.3 %collective-permute-done.54 = bf16[128,2304]{1,0:T(8,128)(2,1)S(1)} collective-permute-done((bf16[128,2304]{1,0:T(8,128)(2,1)S(1)}, bf16[128,2304]{1,0:T(8,128)(2,1)S(1)}, u32[]{:S(2)}, u32[]{:S(2)}) %collective-permute-start.54) | collective-permute-done | bytes 589856 | tf_op jit(solution)/shard_map/ppermute | solution.py:404
  (185 shorter events, 96.5 us)
Async XLA Ops:
  6.5 134.8 %all-gather.2.cloned.1.call-start = ((), (), s32[]{:S(2)}) async-start(), calls=%async_computation | async-start | bytes 2359296 | tf_op jit(solution)/shard_map/all_gather | solution.py:515
  8.0 28.9 %collective-permute-start.5 = (bf16[128,2304]{1,0:T(8,128)(2,1)S(1)}, bf16[128,2304]{1,0:T(8,128)(2,1)S(1)}, u32[]{:S(2)}, u32[]{:S(2)}) collective-permute-start(bf16[128,2304]{1,0:T(8,128)(2,1)S(1)} %get-tuple-element.100.refs_0_), channel_id=1, source_target_pairs={{0,2},{1,3},{2,0},{3,1},{4,6},{5,7},{6,4},{7,5},{8,10},{9,11},{10,... | collective-permute-start | bytes 1769480 | tf_op jit(solution)/shard_map/ppermute | solution.py:385
  11.0 28.6 %collective-permute-start.6 = (bf16[128,2304]{1,0:T(8,128)(2,1)S(1)}, bf16[128,2304]{1,0:T(8,128)(2,1)S(1)}, u32[]{:S(2)}, u32[]{:S(2)}) collective-permute-start(bf16[128,2304]{1,0:T(8,128)(2,1)S(1)} %get-tuple-element.100.refs_0_), channel_id=1, source_target_pairs={{0,4},{1,5},{2,6},{3,7},{4,0},{5,1},{6,2},{7,3},{8,12},{9,13},{10,... | collective-permute-start | bytes 1769480 | tf_op jit(solution)/shard_map/ppermute | solution.py:385
  18.6 21.3 %collective-permute-start.2 = (f32[2,2,256]{2,1,0:T(2,128)S(1)}, f32[2,2,256]{2,1,0:T(2,128)S(1)}, u32[]{:S(2)}, u32[]{:S(2)}) collective-permute-start(f32[2,2,256]{2,1,0:T(2,128)S(1)} %pad_maximum_fusion.2), channel_id=1, source_target_pairs={{0,2},{1,3},{2,0},{3,1},{4,6},{5,7},{6,4},{7,5},{8,10},{9,11},{10,... | collective-permute-start | bytes 12296 | tf_op jit(solution)/shard_map/ppermute | solution.py:385
  19.2 20.8 %collective-permute-start.3 = (f32[2,2,256]{2,1,0:T(2,128)S(1)}, f32[2,2,256]{2,1,0:T(2,128)S(1)}, u32[]{:S(2)}, u32[]{:S(2)}) collective-permute-start(f32[2,2,256]{2,1,0:T(2,128)S(1)} %pad_maximum_fusion.2), channel_id=1, source_target_pairs={{0,4},{1,5},{2,6},{3,7},{4,0},{5,1},{6,2},{7,3},{8,12},{9,13},{10,... | collective-permute-start | bytes 12296 | tf_op jit(solution)/shard_map/ppermute | solution.py:385
  19.2 20.8 %collective-permute-start.4 = (f32[2,2,256]{2,1,0:T(2,128)S(1)}, f32[2,2,256]{2,1,0:T(2,128)S(1)}, u32[]{:S(2)}, u32[]{:S(2)}) collective-permute-start(f32[2,2,256]{2,1,0:T(2,128)S(1)} %pad_maximum_fusion.2), channel_id=1, source_target_pairs={{0,6},{1,7},{2,4},{3,5},{4,2},{5,3},{6,0},{7,1},{8,14},{9,15},{10,... | collective-permute-start | bytes 12296 | tf_op jit(solution)/shard_map/ppermute | solution.py:385
  54.1 16.3 %collective-permute-start.8 = (bf16[128,2304]{1,0:T(8,128)(2,1)S(1)}, bf16[128,2304]{1,0:T(8,128)(2,1)S(1)}, u32[]{:S(2)}, u32[]{:S(2)}) collective-permute-start(bf16[128,2304]{1,0:T(8,128)(2,1)S(1)} %get-tuple-element.98), channel_id=1, source_target_pairs={{0,8},{8,0},{16,24},{24,16},{1,9},{9,1},{17,25},{25,17},{2,10},{10... | collective-permute-start | bytes 1769480 | tf_op jit(solution)/shard_map/ppermute | solution.py:404
  57.5 22.7 %collective-permute-start.10 = (bf16[128,2304]{1,0:T(8,128)(2,1)S(1)}, bf16[128,2304]{1,0:T(8,128)(2,1)S(1)}, u32[]{:S(2)}, u32[]{:S(2)}) collective-permute-start(bf16[128,2304]{1,0:T(8,128)(2,1)S(1)} %get-tuple-element.105), channel_id=1, source_target_pairs={{0,24},{8,16},{16,8},{24,0},{1,25},{9,17},{17,9},{25,1},{2,26},{10... | collective-permute-start | bytes 1769480 | tf_op jit(solution)/shard_map/ppermute | solution.py:404
  59.0 22.9 %collective-permute-start.11 = (bf16[128,2304]{1,0:T(8,128)(2,1)S(1)}, bf16[128,2304]{1,0:T(8,128)(2,1)S(1)}, u32[]{:S(2)}, u32[]{:S(2)}) collective-permute-start(bf16[128,2304]{1,0:T(8,128)(2,1)S(1)} %get-tuple-element.120.refs_0_), channel_id=1, source_target_pairs={{0,2},{1,3},{2,0},{3,1},{4,6},{5,7},{6,4},{7,5},{8,10},{9,11},{10,... | collective-permute-start | bytes 1769480 | tf_op jit(solution)/shard_map/ppermute | solution.py:385
  60.7 25.9 %collective-permute-start.12 = (bf16[128,2304]{1,0:T(8,128)(2,1)S(1)}, bf16[128,2304]{1,0:T(8,128)(2,1)S(1)}, u32[]{:S(2)}, u32[]{:S(2)}) collective-permute-start(bf16[128,2304]{1,0:T(8,128)(2,1)S(1)} %get-tuple-element.120.refs_0_), channel_id=1, source_target_pairs={{0,4},{1,5},{2,6},{3,7},{4,0},{5,1},{6,2},{7,3},{8,12},{9,13},{10,... | collective-permute-start | bytes 1769480 | tf_op jit(solution)/shard_map/ppermute | solution.py:385
  62.1 25.0 %collective-permute-start.9 = (bf16[128,2304]{1,0:T(8,128)(2,1)S(1)}, bf16[128,2304]{1,0:T(8,128)(2,1)S(1)}, u32[]{:S(2)}, u32[]{:S(2)}) collective-permute-start(bf16[128,2304]{1,0:T(8,128)(2,1)S(1)} %get-tuple-element.99), channel_id=1, source_target_pairs={{0,16},{8,24},{16,0},{24,8},{1,17},{9,25},{17,1},{25,9},{2,18},{10... | collective-permute-start | bytes 1769480 | tf_op jit(solution)/shard_map/ppermute | solution.py:404
  70.5 16.7 %collective-permute-start.13 = (bf16[128,2304]{1,0:T(8,128)(2,1)S(1)}, bf16[128,2304]{1,0:T(8,128)(2,1)S(1)}, u32[]{:S(2)}, u32[]{:S(2)}) collective-permute-start(bf16[128,2304]{1,0:T(8,128)(2,1)S(1)} %get-tuple-element.108.refs_0_), channel_id=1, source_target_pairs={{0,1},{1,0},{2,3},{3,2},{4,5},{5,4},{6,7},{7,6},{8,9},{9,8},{10,11... | collective-permute-start | bytes 1769480 | tf_op jit(solution)/shard_map/ppermute | solution.py:421
  87.1 15.7 %collective-permute-start.20 = (bf16[128,2304]{1,0:T(8,128)(2,1)S(1)}, bf16[128,2304]{1,0:T(8,128)(2,1)S(1)}, u32[]{:S(2)}, u32[]{:S(2)}) collective-permute-start(bf16[128,2304]{1,0:T(8,128)(2,1)S(1)} %collective-permute-done.12.refs_2_), channel_id=1, source_target_pairs={{0,2},{1,3},{2,0},{3,1},{4,6},{5,7},{6,4},{7,5},{8,10},{9,11},{10,... | collective-permute-start | bytes 1769480 | tf_op jit(solution)/shard_map/ppermute | solution.py:385
  107.1 16.3 %collective-permute-start.18 = (bf16[128,1152]{1,0:T(8,128)(2,1)S(1)}, bf16[128,1152]{1,0:T(8,128)(2,1)S(1)}, u32[]{:S(2)}, u32[]{:S(2)}) collective-permute-start(bf16[128,1152]{1,0:T(8,128)(2,1)S(1)} %get-tuple-element.111), channel_id=1, source_target_pairs={{0,16},{8,24},{16,0},{24,8},{1,17},{9,25},{17,1},{25,9},{2,18},{10... | collective-permute-start | bytes 884744 | tf_op jit(solution)/shard_map/ppermute | solution.py:404
  107.6 15.8 %collective-permute-start.19 = (bf16[128,1152]{1,0:T(8,128)(2,1)S(1)}, bf16[128,1152]{1,0:T(8,128)(2,1)S(1)}, u32[]{:S(2)}, u32[]{:S(2)}) collective-permute-start(bf16[128,1152]{1,0:T(8,128)(2,1)S(1)} %get-tuple-element.112), channel_id=1, source_target_pairs={{0,24},{8,16},{16,8},{24,0},{1,25},{9,17},{17,9},{25,1},{2,26},{10... | collective-permute-start | bytes 884744 | tf_op jit(solution)/shard_map/ppermute | solution.py:404
  109.1 40.1 %collective-permute-start.30 = (bf16[128,2304]{1,0:T(8,128)(2,1)}, bf16[128,2304]{1,0:T(8,128)(2,1)S(1)}, u32[]{:S(2)}, u32[]{:S(2)}) collective-permute-start(bf16[128,2304]{1,0:T(8,128)(2,1)} %get-tuple-element.118), channel_id=1, source_target_pairs={{0,8},{8,0},{16,24},{24,16},{1,9},{9,1},{17,25},{25,17},{2,10},{10... | collective-permute-start | bytes 1769480 | tf_op jit(solution)/shard_map/ppermute | solution.py:404
  110.6 38.6 %collective-permute-start.31 = (bf16[128,2304]{1,0:T(8,128)(2,1)}, bf16[128,2304]{1,0:T(8,128)(2,1)S(1)}, u32[]{:S(2)}, u32[]{:S(2)}) collective-permute-start(bf16[128,2304]{1,0:T(8,128)(2,1)} %get-tuple-element.119), channel_id=1, source_target_pairs={{0,16},{8,24},{16,0},{24,8},{1,17},{9,25},{17,1},{25,9},{2,18},{10... | collective-permute-start | bytes 1769480 | tf_op jit(solution)/shard_map/ppermute | solution.py:404
  130.5 18.8 %collective-permute-start.32 = (bf16[128,2304]{1,0:T(8,128)(2,1)}, bf16[128,2304]{1,0:T(8,128)(2,1)S(1)}, u32[]{:S(2)}, u32[]{:S(2)}) collective-permute-start(bf16[128,2304]{1,0:T(8,128)(2,1)} %get-tuple-element.135), channel_id=1, source_target_pairs={{0,24},{8,16},{16,8},{24,0},{1,25},{9,17},{17,9},{25,1},{2,26},{10... | collective-permute-start | bytes 1769480 | tf_op jit(solution)/shard_map/ppermute | solution.py:404
  195.3 38.5 %collective-permute-start.36 = (bf16[128,2304]{1,0:T(8,128)(2,1)S(1)}, bf16[128,2304]{1,0:T(8,128)(2,1)S(1)}, u32[]{:S(2)}, u32[]{:S(2)}) collective-permute-start(bf16[128,2304]{1,0:T(8,128)(2,1)S(1)} %get-tuple-element.152), channel_id=1, source_target_pairs={{0,8},{8,0},{16,24},{24,16},{1,9},{9,1},{17,25},{25,17},{2,10},{10... | collective-permute-start | bytes 1769480 | tf_op jit(solution)/shard_map/ppermute | solution.py:404
  197.0 36.9 %collective-permute-start.37 = (bf16[128,2304]{1,0:T(8,128)(2,1)S(1)}, bf16[128,2304]{1,0:T(8,128)(2,1)S(1)}, u32[]{:S(2)}, u32[]{:S(2)}) collective-permute-start(bf16[128,2304]{1,0:T(8,128)(2,1)S(1)} %get-tuple-element.153), channel_id=1, source_target_pairs={{0,16},{8,24},{16,0},{24,8},{1,17},{9,25},{17,1},{25,9},{2,18},{10... | collective-permute-start | bytes 1769480 | tf_op jit(solution)/shard_map/ppermute | solution.py:404
  246.3 17.1 %collective-permute-start.38 = (bf16[128,2304]{1,0:T(8,128)(2,1)S(1)}, bf16[128,2304]{1,0:T(8,128)(2,1)S(1)}, u32[]{:S(2)}, u32[]{:S(2)}) collective-permute-start(bf16[128,2304]{1,0:T(8,128)(2,1)S(1)} %get-tuple-element.154), channel_id=1, source_target_pairs={{0,24},{8,16},{16,8},{24,0},{1,25},{9,17},{17,9},{25,1},{2,26},{10... | collective-permute-start | bytes 1769480 | tf_op jit(solution)/shard_map/ppermute | solution.py:404
  257.5 17.6 %collective-permute-start.52 = (bf16[128,2304]{1,0:T(8,128)(2,1)S(1)}, bf16[128,2304]{1,0:T(8,128)(2,1)S(1)}, u32[]{:S(2)}, u32[]{:S(2)}) collective-permute-start(bf16[128,2304]{1,0:T(8,128)(2,1)S(1)} %get-tuple-element.172), channel_id=1, source_target_pairs={{0,8},{8,0},{16,24},{24,16},{1,9},{9,1},{17,25},{25,17},{2,10},{10... | collective-permute-start | bytes 1769480 | tf_op jit(solution)/shard_map/ppermute | solution.py:404
  258.1 17.8 %collective-permute-start.53 = (bf16[128,2304]{1,0:T(8,128)(2,1)S(1)}, bf16[128,2304]{1,0:T(8,128)(2,1)S(1)}, u32[]{:S(2)}, u32[]{:S(2)}) collective-permute-start(bf16[128,2304]{1,0:T(8,128)(2,1)S(1)} %get-tuple-element.173), channel_id=1, source_target_pairs={{0,16},{8,24},{16,0},{24,8},{1,17},{9,25},{17,1},{25,9},{2,18},{10... | collective-permute-start | bytes 1769480 | tf_op jit(solution)/shard_map/ppermute | solution.py:404
  259.4 28.8 %collective-permute-start.54 = (bf16[128,2304]{1,0:T(8,128)(2,1)S(1)}, bf16[128,2304]{1,0:T(8,128)(2,1)S(1)}, u32[]{:S(2)}, u32[]{:S(2)}) collective-permute-start(bf16[128,2304]{1,0:T(8,128)(2,1)S(1)} %get-tuple-element.174), channel_id=1, source_target_pairs={{0,24},{8,16},{16,8},{24,0},{1,25},{9,17},{17,9},{25,1},{2,26},{10... | collective-permute-start | bytes 1769480 | tf_op jit(solution)/shard_map/ppermute | solution.py:404
  (55 other events, 672.9 us)
Sparse Core Ops, SparseCore 0:
  105.7 26.9 all-gather.1

commit v3 on v2

--- a/solution.py
+++ b/solution.py
@@ -259,7 +259,9 @@
             jax.ShapeDtypeStruct((size, total), jnp.bfloat16 if k else jnp.float32) for k in range(groups)
         ],
         compiler_params=pltpu.CompilerParams(vmem_limit_bytes=VMEM),
-        cost_estimate=FREE,
+        cost_estimate=FREE
+        if extra is not None
+        else pl.CostEstimate(flops=8 * groups * size * depth * total, bytes_accessed=0, transcendentals=0),
     )(which, *operands)
 
 
@@ -366,7 +368,9 @@
         ),
         out_shape=jax.ShapeDtypeStruct((size, columns), jnp.bfloat16),
         compiler_params=pltpu.CompilerParams(vmem_limit_bytes=VMEM),
-        cost_estimate=FREE,
+        cost_estimate=pl.CostEstimate(
+            flops=16 * size * columns * (past.shape[0] + fresh), bytes_accessed=0, transcendentals=0
+        ),
     )(info, *(map(in_hbm, queries) if far else queries), *map(in_hbm, operands[parts : parts + 3]), *operands[parts + 3 :])
 
 
@@ -503,8 +507,9 @@
         def fresh(queries):
             return across(tail_sum(queries, pair_columns_here))
 
-        second = around(tie(tokens[0, parts[1]], first[3]))
-        rows = turn(normalised(0, first))
+        picks = normalised(0, first)
+        second = around(tie(tokens[0, parts[1]], picks[0]))
+        rows = turn(picks)
         rows[-1] = tie(rows[-1], second[1:3])
         other = partner(rows, 1)
         partial = times(rows, other, which, w_query, w_keyval, True)
@@ -516,24 +521,18 @@
         rows = turn(picks)
         heads = attend(info, tie(queries, picks[0]), cosine, sine, past, pairs, True)
         first = around(heads)
-
-        rows = tie(rows, first[1:3])
-        other = partner(rows, 2)
-        picks = pick(index, first)
-        first_rows = turn(picks)
-        rows, other = tie((rows, other), picks)
-        partial = times(rows, other, which, w_query, w_keyval)
+        rows = tie(rows, heads)
+        partial = times(rows, partner(rows, 2), which, w_query, w_keyval)
         queries = give(partial)
-
-        rows = tie(first_rows, partial[0])
-        partial = times(rows, partner(rows, 4), which, w_out)
+        pairs.append(fresh(queries))
+        rows = turn(pick(index, tie(first, (queries[1:], pairs[1][1]))))
+        heads = attend(info, queries, cosine, sine, past, pairs)
+        second = around(heads, 3)
+
+        partial = times(tie(rows, heads), partner(tie(rows, heads), 4), which, w_out)
         outs = [give(partial)]
-
-        queries = tie(queries, partial[0])
-        pairs.append(fresh(queries))
-        heads = attend(info, queries, cosine, sine, past, pairs)
-        rows = turn(pick(index, tie(around(heads), outs[0][1:3])))
-        outs.append(give(times(rows, partner(rows, 4), which, w_out)))
+        rows = turn(pick(index, complete(tie(second, partial[0]))))
+        outs.append(give(times(rows, partner(tie(rows, outs[0][1:3]), 4), which, w_out)))
         outs = [collect(o) for o in outs]
         return jnp.concatenate(outs, axis=0)[None]
 

time: 297 us -> 286 us (0.963)
  waiting for transfers between devices: 151 us -> 131 us
  starting transfers between devices: 55.6 us -> 64.1 us
    ppermute x21, waiting for transfers between devices: 79.7 us -> 61.9 us  [hop(): return lax.ppermute(block, 'yz', pairs)]
    ppermute x21, starting transfers between devices: 24.7 us -> 31.9 us  [hop(): return lax.ppermute(block, 'yz', pairs)]
  transfers between devices with their start and end apart: 56 -> 56, of which waited for: 32 -> 26; matrix products, arithmetic and copies ran while one was open for 1% -> 2% of each run, Pallas kernels for 20% -> 20%
where the time goes in v3:
time: 286 us; the launch traced here: 285 us
  waiting for transfers between devices  131 us (46%)
  starting transfers between devices  64.1 us (22%)
  Pallas kernels  63.8 us (22%)
  between operations  14.6 us (5%)
  local copies, waits for them, and re-layouts  7.79 us (3%)
  other arithmetic  3.86 us (1%)
    ppermute x24, waiting for transfers between devices, exchange(): return lax.ppermute(block, 'gx', [(s, s ^ k) for s in range(n_gx)])  64.7 us
    ppermute x21, waiting for transfers between devices, hop(): return lax.ppermute(block, 'yz', pairs)  61.9 us
    pallas_call x4, Pallas kernels, product(): pl.pallas_call(functools.partial(product_kernel, groups, len(other)), gri...  39.5 us
    ppermute x21, starting transfers between devices, hop(): return lax.ppermute(block, 'yz', pairs)  31.9 us
    ppermute x24, starting transfers between devices, exchange(): return lax.ppermute(block, 'gx', [(s, s ^ k) for s in range(n_gx)])  29.8 us
    pallas_call x2, Pallas kernels, attend(): pl.pallas_call(functools.partial(attend_kernel, sizes, at_once, parts), g...  12.9 us
    pallas_call x4, Pallas kernels, normalise(): pl.pallas_call(functools.partial(normalise_kernel, parts), grid_spec=pltp...  8.83 us
  transfers between devices with their start and end apart: 56, of which 26 were waited for; matrix products, arithmetic and copies ran while one was open for 2% of the time, Pallas kernels for 20%

profile of v3, /device:TPU:0, one launch (start us, length us, event | category | flops | bytes accessed | tf_op | source)
XLA Modules:
  0.0 285.5 jit_solution(2186592546433960539)
XLA Ops:
  8.0 3.1 %collective-permute-start.5 = (bf16[128,2304]{1,0:T(8,128)(2,1)S(1)}, bf16[128,2304]{1,0:T(8,128)(2,1)S(1)}, u32[]{:S(2)}, u32[]{:S(2)}) collective-permute-start(bf16[128,2304]{1,0:T(8,128)(2,1)S(1)} %get-tuple-element.97.refs_0_), channel_id=1, source_target_pairs={{0,2},{1,3},{2,0},{3,1},{4,6},{5,7},{6,4},{7,5},{8,10},{9,11},{10,... | collective-permute-start | bytes 1769480 | tf_op jit(solution)/shard_map/ppermute | solution.py:389
  23.2 13.7 %collective-permute-done.5.refs_1_ = bf16[128,2304]{1,0:T(8,128)(2,1)S(1)} collective-permute-done((bf16[128,2304]{1,0:T(8,128)(2,1)S(1)}, bf16[128,2304]{1,0:T(8,128)(2,1)S(1)}, u32[]{:S(2)}, u32[]{:S(2)}) %collective-permute-start.5) | collective-permute-done | bytes 589856 | tf_op jit(solution)/shard_map/ppermute | solution.py:389
  36.9 2.8 collective-permute-done.6.refs_2_
  40.4 12.0 %collective-permute-done.7.refs_3_ = bf16[128,2304]{1,0:T(8,128)(2,1)S(1)} collective-permute-done((bf16[128,2304]{1,0:T(8,128)(2,1)S(1)}, bf16[128,2304]{1,0:T(8,128)(2,1)S(1)}, u32[]{:S(2)}, u32[]{:S(2)}) %collective-permute-start.7) | collective-permute-done | bytes 589856 | tf_op jit(solution)/shard_map/ppermute | solution.py:389
  62.5 16.9 %collective-permute-done.11.refs_1_ = bf16[128,2304]{1,0:T(8,128)(2,1)S(1)} collective-permute-done((bf16[128,2304]{1,0:T(8,128)(2,1)S(1)}, bf16[128,2304]{1,0:T(8,128)(2,1)S(1)}, u32[]{:S(2)}, u32[]{:S(2)}) %collective-permute-start.11) | collective-permute-done | bytes 589856 | tf_op jit(solution)/shard_map/ppermute | solution.py:389
  79.5 4.6 %collective-permute-done.12.refs_2_ = bf16[128,2304]{1,0:T(8,128)(2,1)S(1)} collective-permute-done((bf16[128,2304]{1,0:T(8,128)(2,1)S(1)}, bf16[128,2304]{1,0:T(8,128)(2,1)S(1)}, u32[]{:S(2)}, u32[]{:S(2)}) %collective-permute-start.12) | collective-permute-done | bytes 589856 | tf_op jit(solution)/shard_map/ppermute | solution.py:389
  88.7 11.3 %shard_map.75 = (f32[128,1152]{1,0:T(8,128)S(1)}, bf16[128,1152]{1,0:T(8,128)(2,1)S(1)}, bf16[128,1152]{1,0:T(8,128)(2,1)S(1)}, bf16[128,1152]{1,0:T(8,128)(2,1)S(1)}) custom-call(s32[1]{0:T(128)} %bitcast.which, bf16[128,2304]{1,0:T(8,128)(2,1)} %copy-done.2, bf16[128,2304]{1,0:T(8,128)(2,1)} %copy-done.20, bf16[128,2304]{1,0:T(8,128)(2,1)} %copy-done.21, ...), custom_call_target="tpu_custom_call" | custom-call | tf_op jit(solution)/shard_map/pallas_call | solution.py:249
  100.9 2.7 shard_map.76
  110.2 3.6 %collective-permute-done.17.refs_1_ = bf16[128,1152]{1,0:T(8,128)(2,1)S(1)} collective-permute-done((bf16[128,1152]{1,0:T(8,128)(2,1)}, bf16[128,1152]{1,0:T(8,128)(2,1)S(1)}, u32[]{:S(2)}, u32[]{:S(2)}) %collective-permute-start.17) | collective-permute-done | bytes 294944 | tf_op jit(solution)/shard_map/ppermute | solution.py:408
  113.8 7.7 %collective-permute-done.18.refs_2_ = bf16[128,1152]{1,0:T(8,128)(2,1)S(1)} collective-permute-done((bf16[128,1152]{1,0:T(8,128)(2,1)S(1)}, bf16[128,1152]{1,0:T(8,128)(2,1)S(1)}, u32[]{:S(2)}, u32[]{:S(2)}) %collective-permute-start.18) | collective-permute-done | bytes 294944 | tf_op jit(solution)/shard_map/ppermute | solution.py:408
  125.0 2.6 shard_map.77
  135.3 3.7 %collective-permute-done.23.refs_10_ = bf16[128,128]{1,0:T(8,128)(2,1)S(1)} collective-permute-done((bf16[128,128]{1,0:T(8,128)(2,1)S(1)}, bf16[128,128]{1,0:T(8,128)(2,1)S(1)}, u32[]{:S(2)}, u32[]{:S(2)}) %collective-permute-start.23) | collective-permute-done | bytes 32800 | tf_op jit(solution)/shard_map/ppermute | solution.py:389
  139.0 6.4 %shard_map.79.refs_0_ = bf16[128,1024]{1,0:T(8,128)(2,1)S(1)} custom-call(s32[2]{0:T(128)S(1)} %pad_add_fusion.info, f32[128,1152]{1,0:T(8,128)} %copy-done.7, bf16[128,1152]{1,0:T(8,128)(2,1)} %copy-done.9, bf16[128,1152]{1,0:T(8,128)(2,1)} %copy-done.10, bf16[128,1152]{1,0:T(8,128)(2,1)} %copy-done.11, f32[256,128]{1,0:T(8,128)} %get-tuple-element.182.refs_4_, ...), custom_call_target="tpu_custom_call" | custom-call | flops 4563402752 | tf_op jit(solution)/shard_map/pallas_call | solution.py:355
  150.4 11.0 %shard_map.82 = (f32[128,1152]{1,0:T(8,128)S(1)}, bf16[128,1152]{1,0:T(8,128)(2,1)S(1)}, bf16[128,1152]{1,0:T(8,128)(2,1)S(1)}, bf16[128,1152]{1,0:T(8,128)(2,1)S(1)}) custom-call(s32[1]{0:T(128)} %bitcast.which, bf16[128,2304]{1,0:T(8,128)(2,1)S(1)} %get-tuple-element.129.refs_0_, bf16[128,2304]{1,0:T(8,128)(2,1)S(1)} %collective-permute-done.27.refs_1_, ...), custom_call_target="tpu_custom_call" | custom-call | tf_op jit(solution)/shard_map/pallas_call | solution.py:249
  166.0 5.4 %collective-permute-done.32.refs_1_ = bf16[128,1152]{1,0:T(8,128)(2,1)S(1)} collective-permute-done((bf16[128,1152]{1,0:T(8,128)(2,1)S(1)}, bf16[128,1152]{1,0:T(8,128)(2,1)S(1)}, u32[]{:S(2)}, u32[]{:S(2)}) %collective-permute-start.32) | collective-permute-done | bytes 294944 | tf_op jit(solution)/shard_map/ppermute | solution.py:408
  171.4 6.7 %collective-permute-done.33.refs_2_ = bf16[128,1152]{1,0:T(8,128)(2,1)S(1)} collective-permute-done((bf16[128,1152]{1,0:T(8,128)(2,1)S(1)}, bf16[128,1152]{1,0:T(8,128)(2,1)S(1)}, u32[]{:S(2)}, u32[]{:S(2)}) %collective-permute-start.33) | collective-permute-done | bytes 294944 | tf_op jit(solution)/shard_map/ppermute | solution.py:408
  187.0 6.5 %shard_map.85.refs_0_ = bf16[128,1024]{1,0:T(8,128)(2,1)S(1)} custom-call(s32[2]{0:T(128)S(1)} %pad_add_fusion.info, f32[128,1152]{1,0:T(8,128)S(1)} %get-tuple-element.136.refs_0_, bf16[128,1152]{1,0:T(8,128)(2,1)S(1)} %collective-permute-done.32.refs_1_, bf16[128,1152]{1,0:T(8,128)(2,1)S(1)} %collective-permute-done.33.refs_2_, ...), custom_call_target="tpu_custom_call" | custom-call | flops 4831838208 | tf_op jit(solution)/shard_map/pallas_call | solution.py:355
  199.0 8.6 %shard_map.87 = (f32[128,2304]{1,0:T(8,128)S(1)}, bf16[128,2304]{1,0:T(8,128)(2,1)S(1)}, bf16[128,2304]{1,0:T(8,128)(2,1)S(1)}, bf16[128,2304]{1,0:T(8,128)(2,1)S(1)}) custom-call(s32[1]{0:T(128)} %bitcast.which, bf16[128,1024]{1,0:T(8,128)(2,1)S(1)} %get-tuple-element.145.refs_0_, bf16[128,1024]{1,0:T(8,128)(2,1)S(1)} %collective-permute-done.36.refs_1_, ...), custom_call_target="tpu_custom_call" | custom-call | flops 9663676416 | tf_op jit(solution)/shard_map/pallas_call | solution.py:249
  212.2 6.1 %collective-permute-done.47.refs_3_ = bf16[128,1024]{1,0:T(8,128)(2,1)S(1)} collective-permute-done((bf16[128,1024]{1,0:T(8,128)(2,1)S(1)}, bf16[128,1024]{1,0:T(8,128)(2,1)S(1)}, u32[]{:S(2)}, u32[]{:S(2)}) %collective-permute-start.47) | collective-permute-done | bytes 262176 | tf_op jit(solution)/shard_map/ppermute | solution.py:389
  223.2 6.3 %collective-permute-done.48.refs_1_ = bf16[128,1024]{1,0:T(8,128)(2,1)S(1)} collective-permute-done((bf16[128,1024]{1,0:T(8,128)(2,1)S(1)}, bf16[128,1024]{1,0:T(8,128)(2,1)S(1)}, u32[]{:S(2)}, u32[]{:S(2)}) %collective-permute-start.48) | collective-permute-done | bytes 262176 | tf_op jit(solution)/shard_map/ppermute | solution.py:408
  229.5 5.6 %collective-permute-done.49.refs_2_ = bf16[128,1024]{1,0:T(8,128)(2,1)S(1)} collective-permute-done((bf16[128,1024]{1,0:T(8,128)(2,1)S(1)}, bf16[128,1024]{1,0:T(8,128)(2,1)S(1)}, u32[]{:S(2)}, u32[]{:S(2)}) %collective-permute-start.49) | collective-permute-done | bytes 262176 | tf_op jit(solution)/shard_map/ppermute | solution.py:408
  238.0 8.6 %shard_map.90 = (f32[128,2304]{1,0:T(8,128)S(1)}, bf16[128,2304]{1,0:T(8,128)(2,1)S(1)}, bf16[128,2304]{1,0:T(8,128)(2,1)S(1)}, bf16[128,2304]{1,0:T(8,128)(2,1)S(1)}) custom-call(s32[1]{0:T(128)} %bitcast.which, bf16[128,1024]{1,0:T(8,128)(2,1)S(1)} %get-tuple-element.161.refs_0_, bf16[128,1024]{1,0:T(8,128)(2,1)S(1)} %collective-permute-done.48.refs_1_, ...), custom_call_target="tpu_custom_call" | custom-call | flops 9663676416 | tf_op jit(solution)/shard_map/pallas_call | solution.py:249
  252.8 12.3 %collective-permute-done.54 = bf16[128,2304]{1,0:T(8,128)(2,1)S(1)} collective-permute-done((bf16[128,2304]{1,0:T(8,128)(2,1)S(1)}, bf16[128,2304]{1,0:T(8,128)(2,1)S(1)}, u32[]{:S(2)}, u32[]{:S(2)}) %collective-permute-start.54) | collective-permute-done | bytes 589856 | tf_op jit(solution)/shard_map/ppermute | solution.py:408
  265.1 12.1 %collective-permute-done.53 = bf16[128,2304]{1,0:T(8,128)(2,1)S(1)} collective-permute-done((bf16[128,2304]{1,0:T(8,128)(2,1)S(1)}, bf16[128,2304]{1,0:T(8,128)(2,1)S(1)}, u32[]{:S(2)}, u32[]{:S(2)}) %collective-permute-start.53) | collective-permute-done | bytes 589856 | tf_op jit(solution)/shard_map/ppermute | solution.py:408
  (183 shorter events, 90.5 us)
Async XLA Ops:
  6.5 132.5 %all-gather.2.cloned.1.call-start = ((), (), s32[]{:S(2)}) async-start(), calls=%async_computation | async-start | bytes 2359296 | tf_op jit(solution)/shard_map/all_gather | solution.py:520
  8.0 28.9 %collective-permute-start.5 = (bf16[128,2304]{1,0:T(8,128)(2,1)S(1)}, bf16[128,2304]{1,0:T(8,128)(2,1)S(1)}, u32[]{:S(2)}, u32[]{:S(2)}) collective-permute-start(bf16[128,2304]{1,0:T(8,128)(2,1)S(1)} %get-tuple-element.97.refs_0_), channel_id=1, source_target_pairs={{0,2},{1,3},{2,0},{3,1},{4,6},{5,7},{6,4},{7,5},{8,10},{9,11},{10,... | collective-permute-start | bytes 1769480 | tf_op jit(solution)/shard_map/ppermute | solution.py:389
  11.0 28.6 %collective-permute-start.6 = (bf16[128,2304]{1,0:T(8,128)(2,1)S(1)}, bf16[128,2304]{1,0:T(8,128)(2,1)S(1)}, u32[]{:S(2)}, u32[]{:S(2)}) collective-permute-start(bf16[128,2304]{1,0:T(8,128)(2,1)S(1)} %get-tuple-element.97.refs_0_), channel_id=1, source_target_pairs={{0,4},{1,5},{2,6},{3,7},{4,0},{5,1},{6,2},{7,3},{8,12},{9,13},{10,... | collective-permute-start | bytes 1769480 | tf_op jit(solution)/shard_map/ppermute | solution.py:389
  18.7 21.3 %collective-permute-start.4 = (f32[2,2,256]{2,1,0:T(2,128)S(1)}, f32[2,2,256]{2,1,0:T(2,128)S(1)}, u32[]{:S(2)}, u32[]{:S(2)}) collective-permute-start(f32[2,2,256]{2,1,0:T(2,128)S(1)} %pad_maximum_fusion.2), channel_id=1, source_target_pairs={{0,6},{1,7},{2,4},{3,5},{4,2},{5,3},{6,0},{7,1},{8,14},{9,15},{10,... | collective-permute-start | bytes 12296 | tf_op jit(solution)/shard_map/ppermute | solution.py:389
  18.7 21.2 %collective-permute-start.3 = (f32[2,2,256]{2,1,0:T(2,128)S(1)}, f32[2,2,256]{2,1,0:T(2,128)S(1)}, u32[]{:S(2)}, u32[]{:S(2)}) collective-permute-start(f32[2,2,256]{2,1,0:T(2,128)S(1)} %pad_maximum_fusion.2), channel_id=1, source_target_pairs={{0,4},{1,5},{2,6},{3,7},{4,0},{5,1},{6,2},{7,3},{8,12},{9,13},{10,... | collective-permute-start | bytes 12296 | tf_op jit(solution)/shard_map/ppermute | solution.py:389
  20.6 19.3 %collective-permute-start.2 = (f32[2,2,256]{2,1,0:T(2,128)S(1)}, f32[2,2,256]{2,1,0:T(2,128)S(1)}, u32[]{:S(2)}, u32[]{:S(2)}) collective-permute-start(f32[2,2,256]{2,1,0:T(2,128)S(1)} %pad_maximum_fusion.2), channel_id=1, source_target_pairs={{0,2},{1,3},{2,0},{3,1},{4,6},{5,7},{6,4},{7,5},{8,10},{9,11},{10,... | collective-permute-start | bytes 12296 | tf_op jit(solution)/shard_map/ppermute | solution.py:389
  55.9 23.5 %collective-permute-start.11 = (bf16[128,2304]{1,0:T(8,128)(2,1)S(1)}, bf16[128,2304]{1,0:T(8,128)(2,1)S(1)}, u32[]{:S(2)}, u32[]{:S(2)}) collective-permute-start(bf16[128,2304]{1,0:T(8,128)(2,1)S(1)} %get-tuple-element.117.refs_0_), channel_id=1, source_target_pairs={{0,2},{1,3},{2,0},{3,1},{4,6},{5,7},{6,4},{7,5},{8,10},{9,11},{10,... | collective-permute-start | bytes 1769480 | tf_op jit(solution)/shard_map/ppermute | solution.py:389
  57.6 26.4 %collective-permute-start.12 = (bf16[128,2304]{1,0:T(8,128)(2,1)S(1)}, bf16[128,2304]{1,0:T(8,128)(2,1)S(1)}, u32[]{:S(2)}, u32[]{:S(2)}) collective-permute-start(bf16[128,2304]{1,0:T(8,128)(2,1)S(1)} %get-tuple-element.117.refs_0_), channel_id=1, source_target_pairs={{0,4},{1,5},{2,6},{3,7},{4,0},{5,1},{6,2},{7,3},{8,12},{9,13},{10,... | collective-permute-start | bytes 1769480 | tf_op jit(solution)/shard_map/ppermute | solution.py:389
  59.0 25.0 %collective-permute-start.10 = (bf16[128,2304]{1,0:T(8,128)(2,1)S(1)}, bf16[128,2304]{1,0:T(8,128)(2,1)S(1)}, u32[]{:S(2)}, u32[]{:S(2)}) collective-permute-start(bf16[128,2304]{1,0:T(8,128)(2,1)S(1)} %get-tuple-element.102), channel_id=1, source_target_pairs={{0,24},{8,16},{16,8},{24,0},{1,25},{9,17},{17,9},{25,1},{2,26},{10... | collective-permute-start | bytes 1769480 | tf_op jit(solution)/shard_map/ppermute | solution.py:408
  61.5 22.7 %collective-permute-start.8 = (bf16[128,2304]{1,0:T(8,128)(2,1)S(1)}, bf16[128,2304]{1,0:T(8,128)(2,1)S(1)}, u32[]{:S(2)}, u32[]{:S(2)}) collective-permute-start(bf16[128,2304]{1,0:T(8,128)(2,1)S(1)} %get-tuple-element.95), channel_id=1, source_target_pairs={{0,8},{8,0},{16,24},{24,16},{1,9},{9,1},{17,25},{25,17},{2,10},{10... | collective-permute-start | bytes 1769480 | tf_op jit(solution)/shard_map/ppermute | solution.py:408
  62.0 22.7 %collective-permute-start.9 = (bf16[128,2304]{1,0:T(8,128)(2,1)S(1)}, bf16[128,2304]{1,0:T(8,128)(2,1)S(1)}, u32[]{:S(2)}, u32[]{:S(2)}) collective-permute-start(bf16[128,2304]{1,0:T(8,128)(2,1)S(1)} %get-tuple-element.96), channel_id=1, source_target_pairs={{0,16},{8,24},{16,0},{24,8},{1,17},{9,25},{17,1},{25,9},{2,18},{10... | collective-permute-start | bytes 1769480 | tf_op jit(solution)/shard_map/ppermute | solution.py:408
  105.2 16.2 %collective-permute-start.18 = (bf16[128,1152]{1,0:T(8,128)(2,1)S(1)}, bf16[128,1152]{1,0:T(8,128)(2,1)S(1)}, u32[]{:S(2)}, u32[]{:S(2)}) collective-permute-start(bf16[128,1152]{1,0:T(8,128)(2,1)S(1)} %get-tuple-element.108), channel_id=1, source_target_pairs={{0,16},{8,24},{16,0},{24,8},{1,17},{9,25},{17,1},{25,9},{2,18},{10... | collective-permute-start | bytes 884744 | tf_op jit(solution)/shard_map/ppermute | solution.py:408
  107.2 38.2 %collective-permute-start.27 = (bf16[128,2304]{1,0:T(8,128)(2,1)}, bf16[128,2304]{1,0:T(8,128)(2,1)S(1)}, u32[]{:S(2)}, u32[]{:S(2)}) collective-permute-start(bf16[128,2304]{1,0:T(8,128)(2,1)} %get-tuple-element.115), channel_id=1, source_target_pairs={{0,8},{8,0},{16,24},{24,16},{1,9},{9,1},{17,25},{25,17},{2,10},{10... | collective-permute-start | bytes 1769480 | tf_op jit(solution)/shard_map/ppermute | solution.py:408
  108.7 36.7 %collective-permute-start.28 = (bf16[128,2304]{1,0:T(8,128)(2,1)}, bf16[128,2304]{1,0:T(8,128)(2,1)S(1)}, u32[]{:S(2)}, u32[]{:S(2)}) collective-permute-start(bf16[128,2304]{1,0:T(8,128)(2,1)} %get-tuple-element.116), channel_id=1, source_target_pairs={{0,16},{8,24},{16,0},{24,8},{1,17},{9,25},{17,1},{25,9},{2,18},{10... | collective-permute-start | bytes 1769480 | tf_op jit(solution)/shard_map/ppermute | solution.py:408
  127.7 17.9 %collective-permute-start.29 = (bf16[128,2304]{1,0:T(8,128)(2,1)}, bf16[128,2304]{1,0:T(8,128)(2,1)S(1)}, u32[]{:S(2)}, u32[]{:S(2)}) collective-permute-start(bf16[128,2304]{1,0:T(8,128)(2,1)} %get-tuple-element.128), channel_id=1, source_target_pairs={{0,24},{8,16},{16,8},{24,0},{1,25},{9,17},{17,9},{25,1},{2,26},{10... | collective-permute-start | bytes 1769480 | tf_op jit(solution)/shard_map/ppermute | solution.py:408
  146.7 18.3 %collective-permute-start.24 = (bf16[128,1024]{1,0:T(8,128)(2,1)S(1)}, bf16[128,1024]{1,0:T(8,128)(2,1)S(1)}, u32[]{:S(2)}, u32[]{:S(2)}) collective-permute-start(bf16[128,1024]{1,0:T(8,128)(2,1)S(1)} %shard_map.79.refs_0_), channel_id=1, source_target_pairs={{0,2},{1,3},{2,0},{3,1},{4,6},{5,7},{6,4},{7,5},{8,10},{9,11},{10,... | collective-permute-start | bytes 786440 | tf_op jit(solution)/shard_map/ppermute | solution.py:389
  147.4 17.7 %collective-permute-start.25 = (bf16[128,1024]{1,0:T(8,128)(2,1)S(1)}, bf16[128,1024]{1,0:T(8,128)(2,1)S(1)}, u32[]{:S(2)}, u32[]{:S(2)}) collective-permute-start(bf16[128,1024]{1,0:T(8,128)(2,1)S(1)} %shard_map.79.refs_0_), channel_id=1, source_target_pairs={{0,4},{1,5},{2,6},{3,7},{4,0},{5,1},{6,2},{7,3},{8,12},{9,13},{10,... | collective-permute-start | bytes 786440 | tf_op jit(solution)/shard_map/ppermute | solution.py:389
  165.0 17.6 %collective-permute-start.26 = (bf16[128,1024]{1,0:T(8,128)(2,1)S(1)}, bf16[128,1024]{1,0:T(8,128)(2,1)S(1)}, u32[]{:S(2)}, u32[]{:S(2)}) collective-permute-start(bf16[128,1024]{1,0:T(8,128)(2,1)S(1)} %collective-permute-done.25.refs_2_), channel_id=1, source_target_pairs={{0,2},{1,3},{2,0},{3,1},{4,6},{5,7},{6,4},{7,5},{8,10},{9,11},{10,... | collective-permute-start | bytes 786440 | tf_op jit(solution)/shard_map/ppermute | solution.py:389
  207.6 27.5 %collective-permute-start.42 = (bf16[128,2304]{1,0:T(8,128)(2,1)S(1)}, bf16[128,2304]{1,0:T(8,128)(2,1)S(1)}, u32[]{:S(2)}, u32[]{:S(2)}) collective-permute-start(bf16[128,2304]{1,0:T(8,128)(2,1)S(1)} %get-tuple-element.150), channel_id=1, source_target_pairs={{0,8},{8,0},{16,24},{24,16},{1,9},{9,1},{17,25},{25,17},{2,10},{10... | collective-permute-start | bytes 1769480 | tf_op jit(solution)/shard_map/ppermute | solution.py:408
  208.8 26.3 %collective-permute-start.43 = (bf16[128,2304]{1,0:T(8,128)(2,1)S(1)}, bf16[128,2304]{1,0:T(8,128)(2,1)S(1)}, u32[]{:S(2)}, u32[]{:S(2)}) collective-permute-start(bf16[128,2304]{1,0:T(8,128)(2,1)S(1)} %get-tuple-element.151), channel_id=1, source_target_pairs={{0,16},{8,24},{16,0},{24,8},{1,17},{9,25},{17,1},{25,9},{2,18},{10... | collective-permute-start | bytes 1769480 | tf_op jit(solution)/shard_map/ppermute | solution.py:408
  235.4 17.2 %collective-permute-start.44 = (bf16[128,2304]{1,0:T(8,128)(2,1)S(1)}, bf16[128,2304]{1,0:T(8,128)(2,1)S(1)}, u32[]{:S(2)}, u32[]{:S(2)}) collective-permute-start(bf16[128,2304]{1,0:T(8,128)(2,1)S(1)} %get-tuple-element.152), channel_id=1, source_target_pairs={{0,24},{8,16},{16,8},{24,0},{1,25},{9,17},{17,9},{25,1},{2,26},{10... | collective-permute-start | bytes 1769480 | tf_op jit(solution)/shard_map/ppermute | solution.py:408
  246.6 18.6 %collective-permute-start.54 = (bf16[128,2304]{1,0:T(8,128)(2,1)S(1)}, bf16[128,2304]{1,0:T(8,128)(2,1)S(1)}, u32[]{:S(2)}, u32[]{:S(2)}) collective-permute-start(bf16[128,2304]{1,0:T(8,128)(2,1)S(1)} %get-tuple-element.168), channel_id=1, source_target_pairs={{0,24},{8,16},{16,8},{24,0},{1,25},{9,17},{17,9},{25,1},{2,26},{10... | collective-permute-start | bytes 1769480 | tf_op jit(solution)/shard_map/ppermute | solution.py:408
  248.1 29.2 %collective-permute-start.53 = (bf16[128,2304]{1,0:T(8,128)(2,1)S(1)}, bf16[128,2304]{1,0:T(8,128)(2,1)S(1)}, u32[]{:S(2)}, u32[]{:S(2)}) collective-permute-start(bf16[128,2304]{1,0:T(8,128)(2,1)S(1)} %get-tuple-element.167), channel_id=1, source_target_pairs={{0,16},{8,24},{16,0},{24,8},{1,17},{9,25},{17,1},{25,9},{2,18},{10... | collective-permute-start | bytes 1769480 | tf_op jit(solution)/shard_map/ppermute | solution.py:408
  248.7 28.5 %collective-permute-start.52 = (bf16[128,2304]{1,0:T(8,128)(2,1)S(1)}, bf16[128,2304]{1,0:T(8,128)(2,1)S(1)}, u32[]{:S(2)}, u32[]{:S(2)}) collective-permute-start(bf16[128,2304]{1,0:T(8,128)(2,1)S(1)} %get-tuple-element.166), channel_id=1, source_target_pairs={{0,8},{8,0},{16,24},{24,16},{1,9},{9,1},{17,25},{25,17},{2,10},{10... | collective-permute-start | bytes 1769480 | tf_op jit(solution)/shard_map/ppermute | solution.py:408
  (54 other events, 613.3 us)
Sparse Core Ops, SparseCore 0:
  103.8 28.4 all-gather.1

commit v4 on v3

--- a/solution.py
+++ b/solution.py
@@ -510,7 +510,6 @@
         picks = normalised(0, first)
         second = around(tie(tokens[0, parts[1]], picks[0]))
         rows = turn(picks)
-        rows[-1] = tie(rows[-1], second[1:3])
         other = partner(rows, 1)
         partial = times(rows, other, which, w_query, w_keyval, True)
         queries = give(partial)

time: 286 us -> 284 us (level)
  starting transfers between devices: 64.1 us -> 52.1 us
  waiting for transfers between devices: 131 us -> 142 us
    ppermute x24, waiting for transfers between devices: 64.7 us -> 77.7 us  [exchange(): return lax.ppermute(block, 'gx', [(s, s ^ k) for s in range(n_gx)])]
    ppermute x21, starting transfers between devices: 31.9 us -> 21.4 us  [hop(): return lax.ppermute(block, 'yz', pairs)]
    ppermute x21, waiting for transfers between devices: 61.9 us -> 58.1 us  [hop(): return lax.ppermute(block, 'yz', pairs)]
  transfers between devices with their start and end apart: 56 -> 56, of which waited for: 26 -> 29; matrix products, arithmetic and copies ran while one was open for 2% -> 2% of each run, Pallas kernels for 20% -> 21%
where the time goes in v4:
time: 284 us
  waiting for transfers between devices  142 us (50%)
  Pallas kernels  64.5 us (23%)
  starting transfers between devices  52.1 us (18%)
  between operations  14.6 us (5%)
  local copies, waits for them, and re-layouts  6.87 us (2%)
  other arithmetic  3.83 us (1%)
    ppermute x24, waiting for transfers between devices, exchange(): return lax.ppermute(block, 'gx', [(s, s ^ k) for s in range(n_gx)])  77.7 us
    ppermute x21, waiting for transfers between devices, hop(): return lax.ppermute(block, 'yz', pairs)  58.1 us
    pallas_call x4, Pallas kernels, product(): pl.pallas_call(functools.partial(product_kernel, groups, len(other)), gri...  40.1 us
    ppermute x24, starting transfers between devices, exchange(): return lax.ppermute(block, 'gx', [(s, s ^ k) for s in range(n_gx)])  28.9 us
    ppermute x21, starting transfers between devices, hop(): return lax.ppermute(block, 'yz', pairs)  21.4 us
    pallas_call x2, Pallas kernels, attend(): pl.pallas_call(functools.partial(attend_kernel, sizes, at_once, parts), g...  13 us
    pallas_call x4, Pallas kernels, normalise(): pl.pallas_call(functools.partial(normalise_kernel, parts), grid_spec=pltp...  8.82 us
    ppermute x8, waiting for transfers between devices, partner(): return [lax.ppermute(block, 'yz', swap) for block in rows]  6.03 us
  transfers between devices with their start and end apart: 56, of which 29 were waited for; matrix products, arithmetic and copies ran while one was open for 2% of the time, Pallas kernels for 21%

profile of v4, /device:TPU:0, one launch (start us, length us, event | category | flops | bytes accessed | tf_op | source)
XLA Modules:
  0.0 283.9 jit_solution(2980440248768299119)
XLA Ops:
  8.0 3.1 %collective-permute-start.5 = (bf16[128,2304]{1,0:T(8,128)(2,1)S(1)}, bf16[128,2304]{1,0:T(8,128)(2,1)S(1)}, u32[]{:S(2)}, u32[]{:S(2)}) collective-permute-start(bf16[128,2304]{1,0:T(8,128)(2,1)S(1)} %get-tuple-element.96.refs_0_), channel_id=1, source_target_pairs={{0,2},{1,3},{2,0},{3,1},{4,6},{5,7},{6,4},{7,5},{8,10},{9,11},{10,... | collective-permute-start | bytes 1769480 | tf_op jit(solution)/shard_map/ppermute | solution.py:389
  23.2 13.7 %collective-permute-done.5.refs_1_ = bf16[128,2304]{1,0:T(8,128)(2,1)S(1)} collective-permute-done((bf16[128,2304]{1,0:T(8,128)(2,1)S(1)}, bf16[128,2304]{1,0:T(8,128)(2,1)S(1)}, u32[]{:S(2)}, u32[]{:S(2)}) %collective-permute-start.5) | collective-permute-done | bytes 589856 | tf_op jit(solution)/shard_map/ppermute | solution.py:389
  40.4 12.0 %collective-permute-done.7.refs_3_ = bf16[128,2304]{1,0:T(8,128)(2,1)S(1)} collective-permute-done((bf16[128,2304]{1,0:T(8,128)(2,1)S(1)}, bf16[128,2304]{1,0:T(8,128)(2,1)S(1)}, u32[]{:S(2)}, u32[]{:S(2)}) %collective-permute-start.7) | collective-permute-done | bytes 589856 | tf_op jit(solution)/shard_map/ppermute | solution.py:389
  62.6 7.9 %collective-permute-done.8.refs_1_ = bf16[128,2304]{1,0:T(8,128)(2,1)S(1)} collective-permute-done((bf16[128,2304]{1,0:T(8,128)(2,1)S(1)}, bf16[128,2304]{1,0:T(8,128)(2,1)S(1)}, u32[]{:S(2)}, u32[]{:S(2)}) %collective-permute-start.8) | collective-permute-done | bytes 589856 | tf_op jit(solution)/shard_map/ppermute | solution.py:408
  70.5 8.8 %collective-permute-done.18.refs_1_ = bf16[128,2304]{1,0:T(8,128)(2,1)S(1)} collective-permute-done((bf16[128,2304]{1,0:T(8,128)(2,1)S(1)}, bf16[128,2304]{1,0:T(8,128)(2,1)S(1)}, u32[]{:S(2)}, u32[]{:S(2)}) %collective-permute-start.18) | collective-permute-done | bytes 589856 | tf_op jit(solution)/shard_map/ppermute | solution.py:389
  79.3 5.1 %collective-permute-done.9.refs_2_ = bf16[128,2304]{1,0:T(8,128)(2,1)S(1)} collective-permute-done((bf16[128,2304]{1,0:T(8,128)(2,1)S(1)}, bf16[128,2304]{1,0:T(8,128)(2,1)S(1)}, u32[]{:S(2)}, u32[]{:S(2)}) %collective-permute-start.9) | collective-permute-done | bytes 589856 | tf_op jit(solution)/shard_map/ppermute | solution.py:408
  87.3 12.0 %shard_map.75 = (f32[128,1152]{1,0:T(8,128)S(1)}, bf16[128,1152]{1,0:T(8,128)(2,1)}, bf16[128,1152]{1,0:T(8,128)(2,1)S(1)}, bf16[128,1152]{1,0:T(8,128)(2,1)S(1)}) custom-call(s32[1]{0:T(128)} %bitcast.which, bf16[128,2304]{1,0:T(8,128)(2,1)} %copy-done.2, bf16[128,2304]{1,0:T(8,128)(2,1)} %copy-done.22, bf16[128,2304]{1,0:T(8,128)(2,1)} %copy-done.23, ...), custom_call_target="tpu_custom_call" | custom-call | tf_op jit(solution)/shard_map/pallas_call | solution.py:249
  108.7 4.5 %collective-permute-done.15.refs_1_ = bf16[128,1152]{1,0:T(8,128)(2,1)S(1)} collective-permute-done((bf16[128,1152]{1,0:T(8,128)(2,1)}, bf16[128,1152]{1,0:T(8,128)(2,1)S(1)}, u32[]{:S(2)}, u32[]{:S(2)}) %collective-permute-start.15) | collective-permute-done | bytes 294944 | tf_op jit(solution)/shard_map/ppermute | solution.py:408
  113.2 6.2 %collective-permute-done.16.refs_2_ = bf16[128,1152]{1,0:T(8,128)(2,1)S(1)} collective-permute-done((bf16[128,1152]{1,0:T(8,128)(2,1)S(1)}, bf16[128,1152]{1,0:T(8,128)(2,1)S(1)}, u32[]{:S(2)}, u32[]{:S(2)}) %collective-permute-start.16) | collective-permute-done | bytes 294944 | tf_op jit(solution)/shard_map/ppermute | solution.py:408
  134.1 4.2 %collective-permute-done.23.refs_10_ = bf16[128,128]{1,0:T(8,128)(2,1)S(1)} collective-permute-done((bf16[128,128]{1,0:T(8,128)(2,1)S(1)}, bf16[128,128]{1,0:T(8,128)(2,1)S(1)}, u32[]{:S(2)}, u32[]{:S(2)}) %collective-permute-start.23) | collective-permute-done | bytes 32800 | tf_op jit(solution)/shard_map/ppermute | solution.py:389
  138.3 6.4 %shard_map.79.refs_0_ = bf16[128,1024]{1,0:T(8,128)(2,1)S(1)} custom-call(s32[2]{0:T(128)S(1)} %pad_add_fusion.info, f32[128,1152]{1,0:T(8,128)} %copy-done.7, bf16[128,1152]{1,0:T(8,128)(2,1)} %copy-done.9, bf16[128,1152]{1,0:T(8,128)(2,1)} %copy-done.10, bf16[128,1152]{1,0:T(8,128)(2,1)} %copy-done.11, f32[256,128]{1,0:T(8,128)} %get-tuple-element.180.refs_4_, ...), custom_call_target="tpu_custom_call" | custom-call | flops 4563402752 | tf_op jit(solution)/shard_map/pallas_call | solution.py:355
  149.7 11.0 %shard_map.82 = (f32[128,1152]{1,0:T(8,128)S(1)}, bf16[128,1152]{1,0:T(8,128)(2,1)S(1)}, bf16[128,1152]{1,0:T(8,128)(2,1)S(1)}, bf16[128,1152]{1,0:T(8,128)(2,1)S(1)}) custom-call(s32[1]{0:T(128)} %bitcast.which, bf16[128,2304]{1,0:T(8,128)(2,1)S(1)} %get-tuple-element.127.refs_0_, bf16[128,2304]{1,0:T(8,128)(2,1)S(1)} %collective-permute-done.27.refs_1_, ...), custom_call_target="tpu_custom_call" | custom-call | tf_op jit(solution)/shard_map/pallas_call | solution.py:249
  164.3 6.3 %collective-permute-done.32.refs_1_ = bf16[128,1152]{1,0:T(8,128)(2,1)S(1)} collective-permute-done((bf16[128,1152]{1,0:T(8,128)(2,1)S(1)}, bf16[128,1152]{1,0:T(8,128)(2,1)S(1)}, u32[]{:S(2)}, u32[]{:S(2)}) %collective-permute-start.32) | collective-permute-done | bytes 294944 | tf_op jit(solution)/shard_map/ppermute | solution.py:408
  170.6 5.9 %collective-permute-done.33.refs_2_ = bf16[128,1152]{1,0:T(8,128)(2,1)S(1)} collective-permute-done((bf16[128,1152]{1,0:T(8,128)(2,1)S(1)}, bf16[128,1152]{1,0:T(8,128)(2,1)S(1)}, u32[]{:S(2)}, u32[]{:S(2)}) %collective-permute-start.33) | collective-permute-done | bytes 294944 | tf_op jit(solution)/shard_map/ppermute | solution.py:408
  177.7 3.4 %collective-permute-start.40 = (bf16[128,128]{1,0:T(8,128)(2,1)S(1)}, bf16[128,128]{1,0:T(8,128)(2,1)S(1)}, u32[]{:S(2)}, u32[]{:S(2)}) collective-permute-start(bf16[128,128]{1,0:T(8,128)(2,1)S(1)} %shard_map.83.refs_11_), channel_id=1, source_target_pairs={{0,6},{1,7},{2,4},{3,5},{4,2},{5,3},{6,0},{7,1},{8,14},{9,15},{10,... | collective-permute-start | bytes 98312 | tf_op jit(solution)/shard_map/ppermute | solution.py:389
  185.4 6.6 %shard_map.85.refs_0_ = bf16[128,1024]{1,0:T(8,128)(2,1)S(1)} custom-call(s32[2]{0:T(128)S(1)} %pad_add_fusion.info, f32[128,1152]{1,0:T(8,128)S(1)} %get-tuple-element.134.refs_0_, bf16[128,1152]{1,0:T(8,128)(2,1)S(1)} %collective-permute-done.32.refs_1_, bf16[128,1152]{1,0:T(8,128)(2,1)S(1)} %collective-permute-done.33.refs_2_, ...), custom_call_target="tpu_custom_call" | custom-call | flops 4831838208 | tf_op jit(solution)/shard_map/pallas_call | solution.py:355
  192.0 3.1 %collective-permute-done.37.refs_2_ = bf16[128,1024]{1,0:T(8,128)(2,1)S(1)} collective-permute-done((bf16[128,1024]{1,0:T(8,128)(2,1)S(1)}, bf16[128,1024]{1,0:T(8,128)(2,1)S(1)}, u32[]{:S(2)}, u32[]{:S(2)}) %collective-permute-start.37) | collective-permute-done | bytes 262176 | tf_op jit(solution)/shard_map/ppermute | solution.py:408
  197.9 8.5 %shard_map.87 = (f32[128,2304]{1,0:T(8,128)S(1)}, bf16[128,2304]{1,0:T(8,128)(2,1)S(1)}, bf16[128,2304]{1,0:T(8,128)(2,1)S(1)}, bf16[128,2304]{1,0:T(8,128)(2,1)S(1)}) custom-call(s32[1]{0:T(128)} %bitcast.which, bf16[128,1024]{1,0:T(8,128)(2,1)S(1)} %get-tuple-element.143.refs_0_, bf16[128,1024]{1,0:T(8,128)(2,1)S(1)} %collective-permute-done.36.refs_1_, ...), custom_call_target="tpu_custom_call" | custom-call | flops 9663676416 | tf_op jit(solution)/shard_map/pallas_call | solution.py:249
  210.6 7.8 %collective-permute-done.47.refs_3_ = bf16[128,1024]{1,0:T(8,128)(2,1)S(1)} collective-permute-done((bf16[128,1024]{1,0:T(8,128)(2,1)S(1)}, bf16[128,1024]{1,0:T(8,128)(2,1)S(1)}, u32[]{:S(2)}, u32[]{:S(2)}) %collective-permute-start.47) | collective-permute-done | bytes 262176 | tf_op jit(solution)/shard_map/ppermute | solution.py:389
  222.9 5.8 %collective-permute-done.48.refs_1_ = bf16[128,1024]{1,0:T(8,128)(2,1)S(1)} collective-permute-done((bf16[128,1024]{1,0:T(8,128)(2,1)S(1)}, bf16[128,1024]{1,0:T(8,128)(2,1)S(1)}, u32[]{:S(2)}, u32[]{:S(2)}) %collective-permute-start.48) | collective-permute-done | bytes 262176 | tf_op jit(solution)/shard_map/ppermute | solution.py:408
  228.6 4.9 %collective-permute-done.49.refs_2_ = bf16[128,1024]{1,0:T(8,128)(2,1)S(1)} collective-permute-done((bf16[128,1024]{1,0:T(8,128)(2,1)S(1)}, bf16[128,1024]{1,0:T(8,128)(2,1)S(1)}, u32[]{:S(2)}, u32[]{:S(2)}) %collective-permute-start.49) | collective-permute-done | bytes 262176 | tf_op jit(solution)/shard_map/ppermute | solution.py:408
  236.4 8.5 %shard_map.90 = (f32[128,2304]{1,0:T(8,128)S(1)}, bf16[128,2304]{1,0:T(8,128)(2,1)S(1)}, bf16[128,2304]{1,0:T(8,128)(2,1)S(1)}, bf16[128,2304]{1,0:T(8,128)(2,1)S(1)}) custom-call(s32[1]{0:T(128)} %bitcast.which, bf16[128,1024]{1,0:T(8,128)(2,1)S(1)} %get-tuple-element.159.refs_0_, bf16[128,1024]{1,0:T(8,128)(2,1)S(1)} %collective-permute-done.48.refs_1_, ...), custom_call_target="tpu_custom_call" | custom-call | flops 9663676416 | tf_op jit(solution)/shard_map/pallas_call | solution.py:249
  251.2 12.3 %collective-permute-done.54 = bf16[128,2304]{1,0:T(8,128)(2,1)S(1)} collective-permute-done((bf16[128,2304]{1,0:T(8,128)(2,1)S(1)}, bf16[128,2304]{1,0:T(8,128)(2,1)S(1)}, u32[]{:S(2)}, u32[]{:S(2)}) %collective-permute-start.54) | collective-permute-done | bytes 589856 | tf_op jit(solution)/shard_map/ppermute | solution.py:408
  263.6 12.1 %collective-permute-done.53 = bf16[128,2304]{1,0:T(8,128)(2,1)S(1)} collective-permute-done((bf16[128,2304]{1,0:T(8,128)(2,1)S(1)}, bf16[128,2304]{1,0:T(8,128)(2,1)S(1)}, u32[]{:S(2)}, u32[]{:S(2)}) %collective-permute-start.53) | collective-permute-done | bytes 589856 | tf_op jit(solution)/shard_map/ppermute | solution.py:408
  (189 shorter events, 89.1 us)
Async XLA Ops:
  6.5 131.8 %all-gather.2.cloned.1.call-start = ((), (), s32[]{:S(2)}) async-start(), calls=%async_computation | async-start | bytes 2359296 | tf_op jit(solution)/shard_map/all_gather | solution.py:519
  8.0 28.9 %collective-permute-start.5 = (bf16[128,2304]{1,0:T(8,128)(2,1)S(1)}, bf16[128,2304]{1,0:T(8,128)(2,1)S(1)}, u32[]{:S(2)}, u32[]{:S(2)}) collective-permute-start(bf16[128,2304]{1,0:T(8,128)(2,1)S(1)} %get-tuple-element.96.refs_0_), channel_id=1, source_target_pairs={{0,2},{1,3},{2,0},{3,1},{4,6},{5,7},{6,4},{7,5},{8,10},{9,11},{10,... | collective-permute-start | bytes 1769480 | tf_op jit(solution)/shard_map/ppermute | solution.py:389
  11.0 28.6 %collective-permute-start.6 = (bf16[128,2304]{1,0:T(8,128)(2,1)S(1)}, bf16[128,2304]{1,0:T(8,128)(2,1)S(1)}, u32[]{:S(2)}, u32[]{:S(2)}) collective-permute-start(bf16[128,2304]{1,0:T(8,128)(2,1)S(1)} %get-tuple-element.96.refs_0_), channel_id=1, source_target_pairs={{0,4},{1,5},{2,6},{3,7},{4,0},{5,1},{6,2},{7,3},{8,12},{9,13},{10,... | collective-permute-start | bytes 1769480 | tf_op jit(solution)/shard_map/ppermute | solution.py:389
  18.6 21.3 %collective-permute-start.4 = (f32[2,2,256]{2,1,0:T(2,128)S(1)}, f32[2,2,256]{2,1,0:T(2,128)S(1)}, u32[]{:S(2)}, u32[]{:S(2)}) collective-permute-start(f32[2,2,256]{2,1,0:T(2,128)S(1)} %pad_maximum_fusion.2), channel_id=1, source_target_pairs={{0,6},{1,7},{2,4},{3,5},{4,2},{5,3},{6,0},{7,1},{8,14},{9,15},{10,... | collective-permute-start | bytes 12296 | tf_op jit(solution)/shard_map/ppermute | solution.py:389
  18.7 21.2 %collective-permute-start.3 = (f32[2,2,256]{2,1,0:T(2,128)S(1)}, f32[2,2,256]{2,1,0:T(2,128)S(1)}, u32[]{:S(2)}, u32[]{:S(2)}) collective-permute-start(f32[2,2,256]{2,1,0:T(2,128)S(1)} %pad_maximum_fusion.2), channel_id=1, source_target_pairs={{0,4},{1,5},{2,6},{3,7},{4,0},{5,1},{6,2},{7,3},{8,12},{9,13},{10,... | collective-permute-start | bytes 12296 | tf_op jit(solution)/shard_map/ppermute | solution.py:389
  20.6 19.3 %collective-permute-start.2 = (f32[2,2,256]{2,1,0:T(2,128)S(1)}, f32[2,2,256]{2,1,0:T(2,128)S(1)}, u32[]{:S(2)}, u32[]{:S(2)}) collective-permute-start(f32[2,2,256]{2,1,0:T(2,128)S(1)} %pad_maximum_fusion.2), channel_id=1, source_target_pairs={{0,2},{1,3},{2,0},{3,1},{4,6},{5,7},{6,4},{7,5},{8,10},{9,11},{10,... | collective-permute-start | bytes 12296 | tf_op jit(solution)/shard_map/ppermute | solution.py:389
  54.1 16.3 %collective-permute-start.8 = (bf16[128,2304]{1,0:T(8,128)(2,1)S(1)}, bf16[128,2304]{1,0:T(8,128)(2,1)S(1)}, u32[]{:S(2)}, u32[]{:S(2)}) collective-permute-start(bf16[128,2304]{1,0:T(8,128)(2,1)S(1)} %get-tuple-element.94), channel_id=1, source_target_pairs={{0,8},{8,0},{16,24},{24,16},{1,9},{9,1},{17,25},{25,17},{2,10},{10... | collective-permute-start | bytes 1769480 | tf_op jit(solution)/shard_map/ppermute | solution.py:408
  57.5 21.8 %collective-permute-start.18 = (bf16[128,2304]{1,0:T(8,128)(2,1)S(1)}, bf16[128,2304]{1,0:T(8,128)(2,1)S(1)}, u32[]{:S(2)}, u32[]{:S(2)}) collective-permute-start(bf16[128,2304]{1,0:T(8,128)(2,1)S(1)} %get-tuple-element.115.refs_0_), channel_id=1, source_target_pairs={{0,2},{1,3},{2,0},{3,1},{4,6},{5,7},{6,4},{7,5},{8,10},{9,11},{10,... | collective-permute-start | bytes 1769480 | tf_op jit(solution)/shard_map/ppermute | solution.py:389
  59.2 25.2 %collective-permute-start.9 = (bf16[128,2304]{1,0:T(8,128)(2,1)S(1)}, bf16[128,2304]{1,0:T(8,128)(2,1)S(1)}, u32[]{:S(2)}, u32[]{:S(2)}) collective-permute-start(bf16[128,2304]{1,0:T(8,128)(2,1)S(1)} %get-tuple-element.95), channel_id=1, source_target_pairs={{0,16},{8,24},{16,0},{24,8},{1,17},{9,25},{17,1},{25,9},{2,18},{10... | collective-permute-start | bytes 1769480 | tf_op jit(solution)/shard_map/ppermute | solution.py:408
  60.7 23.7 %collective-permute-start.10 = (bf16[128,2304]{1,0:T(8,128)(2,1)S(1)}, bf16[128,2304]{1,0:T(8,128)(2,1)S(1)}, u32[]{:S(2)}, u32[]{:S(2)}) collective-permute-start(bf16[128,2304]{1,0:T(8,128)(2,1)S(1)} %get-tuple-element.101), channel_id=1, source_target_pairs={{0,24},{8,16},{16,8},{24,0},{1,25},{9,17},{17,9},{25,1},{2,26},{10... | collective-permute-start | bytes 1769480 | tf_op jit(solution)/shard_map/ppermute | solution.py:408
  61.2 25.6 %collective-permute-start.19 = (bf16[128,2304]{1,0:T(8,128)(2,1)S(1)}, bf16[128,2304]{1,0:T(8,128)(2,1)S(1)}, u32[]{:S(2)}, u32[]{:S(2)}) collective-permute-start(bf16[128,2304]{1,0:T(8,128)(2,1)S(1)} %get-tuple-element.115.refs_0_), channel_id=1, source_target_pairs={{0,4},{1,5},{2,6},{3,7},{4,0},{5,1},{6,2},{7,3},{8,12},{9,13},{10,... | collective-permute-start | bytes 1769480 | tf_op jit(solution)/shard_map/ppermute | solution.py:389
  70.5 16.3 %collective-permute-start.11 = (bf16[128,2304]{1,0:T(8,128)(2,1)S(1)}, bf16[128,2304]{1,0:T(8,128)(2,1)S(1)}, u32[]{:S(2)}, u32[]{:S(2)}) collective-permute-start(bf16[128,2304]{1,0:T(8,128)(2,1)S(1)} %get-tuple-element.102.refs_0_), channel_id=1, source_target_pairs={{0,1},{1,0},{2,3},{3,2},{4,5},{5,4},{6,7},{7,6},{8,9},{9,8},{10,11... | collective-permute-start | bytes 1769480 | tf_op jit(solution)/shard_map/ppermute | solution.py:425
  106.5 38.2 %collective-permute-start.27 = (bf16[128,2304]{1,0:T(8,128)(2,1)}, bf16[128,2304]{1,0:T(8,128)(2,1)S(1)}, u32[]{:S(2)}, u32[]{:S(2)}) collective-permute-start(bf16[128,2304]{1,0:T(8,128)(2,1)} %get-tuple-element.113), channel_id=1, source_target_pairs={{0,8},{8,0},{16,24},{24,16},{1,9},{9,1},{17,25},{25,17},{2,10},{10... | collective-permute-start | bytes 1769480 | tf_op jit(solution)/shard_map/ppermute | solution.py:408
  107.2 37.6 %collective-permute-start.28 = (bf16[128,2304]{1,0:T(8,128)(2,1)}, bf16[128,2304]{1,0:T(8,128)(2,1)S(1)}, u32[]{:S(2)}, u32[]{:S(2)}) collective-permute-start(bf16[128,2304]{1,0:T(8,128)(2,1)} %get-tuple-element.114), channel_id=1, source_target_pairs={{0,16},{8,24},{16,0},{24,8},{1,17},{9,25},{17,1},{25,9},{2,18},{10... | collective-permute-start | bytes 1769480 | tf_op jit(solution)/shard_map/ppermute | solution.py:408
  126.6 18.1 %collective-permute-start.29 = (bf16[128,2304]{1,0:T(8,128)(2,1)}, bf16[128,2304]{1,0:T(8,128)(2,1)S(1)}, u32[]{:S(2)}, u32[]{:S(2)}) collective-permute-start(bf16[128,2304]{1,0:T(8,128)(2,1)} %get-tuple-element.126), channel_id=1, source_target_pairs={{0,24},{8,16},{16,8},{24,0},{1,25},{9,17},{17,9},{25,1},{2,26},{10... | collective-permute-start | bytes 1769480 | tf_op jit(solution)/shard_map/ppermute | solution.py:408
  146.0 18.3 %collective-permute-start.24 = (bf16[128,1024]{1,0:T(8,128)(2,1)S(1)}, bf16[128,1024]{1,0:T(8,128)(2,1)S(1)}, u32[]{:S(2)}, u32[]{:S(2)}) collective-permute-start(bf16[128,1024]{1,0:T(8,128)(2,1)S(1)} %shard_map.79.refs_0_), channel_id=1, source_target_pairs={{0,2},{1,3},{2,0},{3,1},{4,6},{5,7},{6,4},{7,5},{8,10},{9,11},{10,... | collective-permute-start | bytes 786440 | tf_op jit(solution)/shard_map/ppermute | solution.py:389
  146.0 18.3 %collective-permute-start.25 = (bf16[128,1024]{1,0:T(8,128)(2,1)S(1)}, bf16[128,1024]{1,0:T(8,128)(2,1)S(1)}, u32[]{:S(2)}, u32[]{:S(2)}) collective-permute-start(bf16[128,1024]{1,0:T(8,128)(2,1)S(1)} %shard_map.79.refs_0_), channel_id=1, source_target_pairs={{0,4},{1,5},{2,6},{3,7},{4,0},{5,1},{6,2},{7,3},{8,12},{9,13},{10,... | collective-permute-start | bytes 786440 | tf_op jit(solution)/shard_map/ppermute | solution.py:389
  164.3 16.8 %collective-permute-start.26 = (bf16[128,1024]{1,0:T(8,128)(2,1)S(1)}, bf16[128,1024]{1,0:T(8,128)(2,1)S(1)}, u32[]{:S(2)}, u32[]{:S(2)}) collective-permute-start(bf16[128,1024]{1,0:T(8,128)(2,1)S(1)} %collective-permute-done.25.refs_2_), channel_id=1, source_target_pairs={{0,2},{1,3},{2,0},{3,1},{4,6},{5,7},{6,4},{7,5},{8,10},{9,11},{10,... | collective-permute-start | bytes 786440 | tf_op jit(solution)/shard_map/ppermute | solution.py:389
  206.5 27.1 %collective-permute-start.42 = (bf16[128,2304]{1,0:T(8,128)(2,1)S(1)}, bf16[128,2304]{1,0:T(8,128)(2,1)S(1)}, u32[]{:S(2)}, u32[]{:S(2)}) collective-permute-start(bf16[128,2304]{1,0:T(8,128)(2,1)S(1)} %get-tuple-element.148), channel_id=1, source_target_pairs={{0,8},{8,0},{16,24},{24,16},{1,9},{9,1},{17,25},{25,17},{2,10},{10... | collective-permute-start | bytes 1769480 | tf_op jit(solution)/shard_map/ppermute | solution.py:408
  207.2 26.4 %collective-permute-start.43 = (bf16[128,2304]{1,0:T(8,128)(2,1)S(1)}, bf16[128,2304]{1,0:T(8,128)(2,1)S(1)}, u32[]{:S(2)}, u32[]{:S(2)}) collective-permute-start(bf16[128,2304]{1,0:T(8,128)(2,1)S(1)} %get-tuple-element.149), channel_id=1, source_target_pairs={{0,16},{8,24},{16,0},{24,8},{1,17},{9,25},{17,1},{25,9},{2,18},{10... | collective-permute-start | bytes 1769480 | tf_op jit(solution)/shard_map/ppermute | solution.py:408
  233.8 17.2 %collective-permute-start.44 = (bf16[128,2304]{1,0:T(8,128)(2,1)S(1)}, bf16[128,2304]{1,0:T(8,128)(2,1)S(1)}, u32[]{:S(2)}, u32[]{:S(2)}) collective-permute-start(bf16[128,2304]{1,0:T(8,128)(2,1)S(1)} %get-tuple-element.150), channel_id=1, source_target_pairs={{0,24},{8,16},{16,8},{24,0},{1,25},{9,17},{17,9},{25,1},{2,26},{10... | collective-permute-start | bytes 1769480 | tf_op jit(solution)/shard_map/ppermute | solution.py:408
  245.0 18.6 %collective-permute-start.54 = (bf16[128,2304]{1,0:T(8,128)(2,1)S(1)}, bf16[128,2304]{1,0:T(8,128)(2,1)S(1)}, u32[]{:S(2)}, u32[]{:S(2)}) collective-permute-start(bf16[128,2304]{1,0:T(8,128)(2,1)S(1)} %get-tuple-element.166), channel_id=1, source_target_pairs={{0,24},{8,16},{16,8},{24,0},{1,25},{9,17},{17,9},{25,1},{2,26},{10... | collective-permute-start | bytes 1769480 | tf_op jit(solution)/shard_map/ppermute | solution.py:408
  246.4 29.3 %collective-permute-start.53 = (bf16[128,2304]{1,0:T(8,128)(2,1)S(1)}, bf16[128,2304]{1,0:T(8,128)(2,1)S(1)}, u32[]{:S(2)}, u32[]{:S(2)}) collective-permute-start(bf16[128,2304]{1,0:T(8,128)(2,1)S(1)} %get-tuple-element.165), channel_id=1, source_target_pairs={{0,16},{8,24},{16,0},{24,8},{1,17},{9,25},{17,1},{25,9},{2,18},{10... | collective-permute-start | bytes 1769480 | tf_op jit(solution)/shard_map/ppermute | solution.py:408
  247.9 27.8 %collective-permute-start.52 = (bf16[128,2304]{1,0:T(8,128)(2,1)S(1)}, bf16[128,2304]{1,0:T(8,128)(2,1)S(1)}, u32[]{:S(2)}, u32[]{:S(2)}) collective-permute-start(bf16[128,2304]{1,0:T(8,128)(2,1)S(1)} %get-tuple-element.164), channel_id=1, source_target_pairs={{0,8},{8,0},{16,24},{24,16},{1,9},{9,1},{17,25},{25,17},{2,10},{10... | collective-permute-start | bytes 1769480 | tf_op jit(solution)/shard_map/ppermute | solution.py:408
  (57 other events, 664.8 us)
Sparse Core Ops, SparseCore 0:
  103.1 28.2 all-gather.1
